TPU v7x, 128 devices: a whole 4x4x4 slice. The times are simulated.
128 devices in a mesh: tm: 8 (over z, core), chan: 16 (over x, y).
Axes of the slice: x: 4, y: 4, z: 4, core: 2. Of those that a mesh axis runs over, the one named last changes fastest.
Arguments:
- records: float32 [2048, 32768], P(None, ('tm', 'chan')), may hold values from -6 to 6
- pairs: int32 [48, 2], replicated, may hold values from 0 to 15, as said below
- owners: int32 [48, 1], replicated, may hold values from 0 to 15; in each aligned block of 48 rows (0 to 47, 48 to 95, ...) at most 6 rows name the same one
- starts: int32 [58], replicated, may hold values from 0 to 31744, as said below
Outputs:
- cross_spectra: bfloat16 [96, 384, 2, 128, 128], P('chan', 'tm')
Inputs may be any that keep to these rules, and one draw needn't show every extreme that they name: `pairs`: each row holds blocks a, b with 0 <= b - a <= 2; every block is the first member of exactly 3 rows. `owners`: no owner holds more than 6 pairs and some owner holds exactly 6; every owner holds at least one. `starts`: the first possible start 0 and the last possible start 32768 - 1024 each occur.
All inputs are finite; a program needn't handle non-finite values.
Results may differ from a plain program's by a relative error of at most 0.0049.
Values may be sent and summed in bfloat16 or wider, within the bound.
A program may use at most 256 MiB of HBM per device.

v0:
```python
import math

import jax
import jax.numpy as jnp
from jax import lax
from jax.sharding import PartitionSpec as P

NFFT = 1024
NFREQ = 384
WBAND = 64
SEG = 58
PMAX = 6


def slot_table(owners, owner_count):
    owner = owners[:, 0]
    npair = owner.shape[0]
    order = jnp.arange(npair, dtype=jnp.int32)
    same = owner[:, None] == owner[None, :]
    before = order[None, :] < order[:, None]
    rank = jnp.sum((same & before).astype(jnp.int32), axis=1)
    target = owner * PMAX + rank
    rows = jnp.arange(owner_count * PMAX, dtype=jnp.int32)
    match = target[None, :] == rows[:, None]
    live = jnp.any(match, axis=1)
    pair_id = jnp.sum(jnp.where(match, order[None, :], 0), axis=1)
    return (pair_id, live)


def dft_table(group_freq):
    column = jnp.arange(2 * NFREQ, dtype=jnp.int32)
    group = column // (2 * group_freq)
    part_index = column // group_freq % 2
    freq = group * group_freq + column % group_freq
    sample = jnp.arange(NFFT, dtype=jnp.int32)
    phase = sample[:, None] * freq[None, :] % NFFT
    angle = 2.0 * jnp.pi * phase.astype(jnp.float32) / NFFT
    return jnp.where(part_index[None, :] == 0, jnp.cos(angle), -jnp.sin(angle))


def cross_block(left, right):
    norm = 1.0 / math.sqrt(SEG)
    turned = jnp.concatenate([-right[:, 1:2], right[:, 0:1]], axis=1)
    dims = (((1, 2), (1, 2)), ((0,), (0,)))
    real_sum = lax.dot_general(left, right, dims, preferred_element_type=jnp.float32)
    imag_sum = lax.dot_general(left, turned, dims, preferred_element_type=jnp.float32)
    return (jnp.stack([real_sum, imag_sum], axis=1) * norm).astype(jnp.bfloat16)


def slot_products(held, my_live, group_freq, block):
    live_count = jnp.sum(my_live.astype(jnp.int32))
    result = jnp.zeros((PMAX, group_freq, 2, block, block), jnp.bfloat16)

    def one_slot(slot, result):
        left = lax.dynamic_index_in_dim(held, 2 * slot, 0, keepdims=False)
        right = lax.dynamic_index_in_dim(held, 2 * slot + 1, 0, keepdims=False)
        product = cross_block(left, right)
        return lax.dynamic_update_slice_in_dim(result, product[None], slot, 0)

    return lax.fori_loop(0, live_count, one_slot, result)


def body(records, pairs, owners, starts):
    tm_count = lax.axis_size("tm")
    chan_count = lax.axis_size("chan")
    chans, samp_dev = records.shape
    block = chans // chan_count
    sub = block // tm_count
    group_freq = NFREQ // tm_count
    moved = records.reshape(chan_count, tm_count, sub, samp_dev).transpose(1, 0, 2, 3)
    moved = moved.reshape(tm_count * chan_count, sub, 1, samp_dev)
    moved = lax.all_to_all(moved, ("tm", "chan"), split_axis=0, concat_axis=2, tiled=True)
    traces = moved.reshape(sub, -1)

    def cut(begin):
        return lax.dynamic_slice_in_dim(traces, begin, NFFT, 1)

    frames = jax.vmap(cut)(starts)
    steps_n = jnp.arange(NFFT).astype(jnp.float32)
    window = 0.5 - 0.5 * jnp.cos(2.0 * jnp.pi * steps_n / NFFT)
    framed = (frames * window).reshape(SEG * sub, NFFT)
    spectrum = jnp.dot(
        framed,
        dft_table(group_freq),
        precision=lax.Precision.HIGHEST,
        preferred_element_type=jnp.float32,
    )
    parts = spectrum.reshape(SEG, sub, tm_count, 2, group_freq)
    power = parts[:, :, :, 0] * parts[:, :, :, 0] + parts[:, :, :, 1] * parts[:, :, :, 1]
    band = jnp.mean(power.reshape(SEG, sub, NFREQ // WBAND, WBAND), axis=-1, keepdims=True)
    band = jnp.broadcast_to(band, (SEG, sub, NFREQ // WBAND, WBAND)).reshape(
        SEG, sub, tm_count, 1, group_freq
    )
    whitened = (
        (parts / jnp.sqrt(band + 1e-06))
        .astype(jnp.bfloat16)
        .reshape(SEG, sub, tm_count, 2 * group_freq)
    )
    pair_id, live = slot_table(owners, chan_count)
    first = pairs[pair_id, 0]
    second = pairs[pair_id, 1]
    me_chan = lax.axis_index("chan")
    my_first = lax.dynamic_slice_in_dim(first, me_chan * PMAX, PMAX)
    my_second = lax.dynamic_slice_in_dim(second, me_chan * PMAX, PMAX)
    my_live = lax.dynamic_slice_in_dim(live, me_chan * PMAX, PMAX)
    needed = jnp.stack([my_first, my_second], axis=1).reshape(2 * PMAX)
    banded = lax.all_to_all(whitened, "tm", split_axis=2, concat_axis=1, tiled=True)
    local = banded.reshape(SEG, block, 2, group_freq).transpose(3, 2, 0, 1)
    holder = jnp.zeros((2 * PMAX,) + local.shape, jnp.bfloat16)
    piece = lax.all_gather(local[None], "chan", axis=0, tiled=True)
    count = piece.shape[0]
    inside = (needed >= 0) & (needed < count)
    picked = piece[jnp.clip(needed, 0, count - 1)]
    held = jnp.where(inside[:, None, None, None, None], picked, holder)
    return slot_products(held, my_live, group_freq, block)


def solution(mesh):
    return jax.shard_map(
        body,
        mesh=mesh,
        in_specs=(P(None, ("tm", "chan")), P(), P(), P()),
        out_specs=P("chan", "tm", None, None, None),
        check_vma=False,
    )
```

profile of v0, /device:TPU:1, one launch (start us, length us, event | category | flops | bytes accessed | tf_op | source)
XLA Modules:
  0.0 600.7 jit_solution(16591840784505593097)
XLA Ops:
  6.5 3.2 copy.45
  9.7 11.5 %all-to-all-start = ((f32[128,16,1,256]{3,1,2,0:T(8,128)}), f32[128,16,1,256]{3,1,2,0:T(8,128)S(1)}, u32[]{:S(2)}, u32[]{:S(2)}) async-start(f32[128,16,1,256]{3,1,2,0:T(8,128)} %bitcast.104), calls=%async_computation | async-start | bytes 4194304 | tf_op jit(solution)/shard_map/all_to_all | solution.py:72
  21.5 29.5 %all-to-all-done = f32[128,16,1,256]{3,1,2,0:T(8,128)S(1)} async-done(((f32[128,16,1,256]{3,1,2,0:T(8,128)}), f32[128,16,1,256]{3,1,2,0:T(8,128)S(1)}, u32[]{:S(2)}, u32[]{:S(2)}) %all-to-all-start) | async-done | bytes 2097184 | tf_op jit(solution)/shard_map/all_to_all | solution.py:72
  52.5 163.4 %while.14 = (s32[]{:T(128)}, f32[16,32768]{1,0:T(8,128)}, s32[58,2]{0,1:T(2,128)S(1)}, f32[58,16,1024]{2,1,0:T(8,128)}, s32[]{:T(128)}) while((s32[]{:T(128)}, f32[16,32768]{1,0:T(8,128)}, s32[58,2]{0,1:T(2,128)S(1)}, f32[58,16,1024]{2,1,0:T(8,128)}, s32[]{:T(128)}) %tuple.50), condition=%wide.while_cond, body=%wide.while_body.sunk | while | flops 2 | bytes 131685 | solution.py:76
  58.8 2.2 bitcast_dynamic-update-slice_fusion.2
  61.6 2.2 bitcast_dynamic-update-slice_fusion.2
  67.2 2.2 bitcast_dynamic-update-slice_fusion.2
  70.0 2.2 bitcast_dynamic-update-slice_fusion.2
  72.8 2.2 bitcast_dynamic-update-slice_fusion.2
  78.5 2.2 bitcast_dynamic-update-slice_fusion.2
  81.3 2.2 bitcast_dynamic-update-slice_fusion.2
  84.1 2.2 bitcast_dynamic-update-slice_fusion.2
  89.8 2.2 bitcast_dynamic-update-slice_fusion.2
  92.6 2.2 bitcast_dynamic-update-slice_fusion.2
  101.0 2.2 bitcast_dynamic-update-slice_fusion.2
  103.8 2.2 bitcast_dynamic-update-slice_fusion.2
  112.3 2.2 bitcast_dynamic-update-slice_fusion.2
  115.1 2.2 bitcast_dynamic-update-slice_fusion.2
  120.7 2.2 bitcast_dynamic-update-slice_fusion.2
  123.6 2.2 bitcast_dynamic-update-slice_fusion.2
  126.4 2.2 bitcast_dynamic-update-slice_fusion.2
  132.0 2.2 bitcast_dynamic-update-slice_fusion.2
  134.8 2.2 bitcast_dynamic-update-slice_fusion.2
  137.7 2.2 bitcast_dynamic-update-slice_fusion.2
  215.9 2.5 fusion.59
  218.4 43.3 %fusion.12 = f32[58,16,8,2,48]{4,1,3,2,0:T(8,128)S(1)} fusion(s32[8,2,48]{2,1,0:T(2,128)S(1)} %fusion.38, pred[8,2,48]{2,1,0:T(4,128)(4,1)S(1)} %fusion.40, f32[58,16,1024,1,1]{2,1,4,3,0:T(8,128)S(1)} %fusion.59), kind=kOutput, calls=%fused_computation.30 | convolution fusion | flops 8770289664 | bytes 6655744 | tf_op jit(solution)/shard_map/dot_general | solution.py:82
  261.7 3.1 copy-done.2
  264.9 2.5 fusion.11
  267.4 4.1 copy.47
  272.3 3.6 copy.48
  275.9 5.7 divide_convert_fusion
  281.6 5.8 copy.60
  287.4 6.3 %reshape.266 = bf16[58,16,8,96]{3,1,0,2:T(8,128)(2,1)S(1)} reshape(bf16[58,16,8,2,48]{4,3,1,0,2:T(2,128)(2,1)} %copy.60) | data formatting | bytes 2850816 | tf_op jit(solution)/shard_map/reshape | solution.py:97
  293.6 28.0 %all_to_all.30 = bf16[58,16,8,96]{3,1,0,2:T(8,128)(2,1)S(1)} all-to-all(bf16[58,16,8,96]{3,1,0,2:T(8,128)(2,1)S(1)} %reshape.266), channel_id=1, replica_groups=mesh['tm'=8,'chan'=16] {'tm'}, dimensions={2} | all-to-all | bytes 2850816 | tf_op jit(solution)/shard_map/all_to_all | solution.py:107
  322.2 3.2 reshape.221
  325.4 10.3 %copy.52 = bf16[48,2,58,128]{3,1,2,0:T(2,128)(2,1)} copy(bf16[48,2,58,128]{0,1,3,2:T(2,128)(2,1)} %bitcast.100) | data formatting | bytes 2850816 | tf_op jit(solution)/shard_map/transpose | solution.py:108
  340.5 133.9 %all-gather.3.cloned.1.call-done = bf16[768,2,58,128]{3,1,2,0:T(2,128)(2,1)} async-done(((bf16[48,2,58,128]{3,1,2,0:T(2,128)(2,1)}), bf16[768,2,58,128]{3,1,2,0:T(2,128)(2,1)}) %all-gather.3.cloned.1.call-update) | async-done | bytes 22806544 | tf_op jit(solution)/shard_map/all_gather | solution.py:110
  474.4 21.8 %copy.55 = bf16[16,48,2,58,128]{4,3,2,1,0:T(8,128)(2,1)} copy(bf16[16,48,2,58,128]{4,2,3,1,0:T(2,128)(2,1)} %bitcast.99) | data formatting | bytes 45613056 | tf_op jit(solution)/shard_map/all_gather | solution.py:110
  496.2 16.6 %gather_fusion.2 = bf16[12,48,2,58,128]{4,3,2,1,0:T(8,128)(2,1)} fusion(bf16[16,48,2,58,128]{4,3,2,1,0:T(8,128)(2,1)} %copy.55, s32[1024]{0:T(1024)S(1)} %pad_clamp_fusion), kind=kCustom, calls=%fused_computation.2 | custom fusion | bytes 34209840 | tf_op jit(solution)/shard_map/gather | solution.py:113
  512.8 16.8 %broadcast_select_fusion = bf16[12,48,2,58,128]{4,3,2,1,0:T(8,128)(2,1)} fusion(bf16[12,48,2,58,128]{4,3,2,1,0:T(8,128)(2,1)} %gather_fusion.2, pred[12]{0:T(512)(128)(4,1)S(1)} %and.64), kind=kLoop, calls=%fused_computation.22 | loop fusion | flops 8552448 | bytes 34209804 | tf_op jit(solution)/shard_map/jit(_where)/select_n | solution.py:114
  529.6 7.0 %broadcast_in_dim.35.clone = bf16[6,48,2,128,128]{4,3,2,1,0:T(8,128)(2,1)} broadcast(bf16[]{:T(256)} %constant.131.clone.1), dimensions={} | broadcast | bytes 18874370 | tf_op jit(solution)/shard_map/broadcast_in_dim | solution.py:52
  536.6 56.2 %while.13 = (s32[]{:T(128)}, bf16[6,48,2,128,128]{4,3,2,1,0:T(8,128)(2,1)}, s32[]{:T(128)}, bf16[12,48,2,58,128]{4,3,2,1,0:T(8,128)(2,1)}, s32[]{:T(128)}, /*ind...) while((s32[]{:T(128)}, bf16[6,48,2,128,128]{4,3,2,1,0:T(8,128)(2,1)}, s32[]{:T(128)}, ...), condition=%wide.region_6.7_spmd, body=%wide.region_5.6_spmd.sunk | while | flops 370692096 | bytes 27427068 | solution.py:60
  543.3 2.6 copy_dynamic-update-slice_fusion.2
  552.5 2.6 copy_dynamic-update-slice_fusion.2
  561.8 2.6 copy_dynamic-update-slice_fusion.2
  571.0 2.6 copy_dynamic-update-slice_fusion.2
  580.3 2.6 copy_dynamic-update-slice_fusion.2
  589.6 2.6 copy_dynamic-update-slice_fusion.2
  (217 shorter events, 162.9 us)
Async XLA Ops:
  6.5 329.5 %copy-start = (s32[48,2]{0,1:T(2,128)S(1)}, s32[48,2]{0,1:T(2,128)}, u32[]{:S(2)}) copy-start(s32[48,2]{0,1:T(2,128)} %param.7) | copy-start | bytes 1156
  6.5 14.8 %copy-start.3 = (s32[58]{0:T(128)S(1)}, s32[58]{0:T(128)}, u32[]{:S(2)}) copy-start(s32[58]{0:T(128)} %param.9) | copy-start | bytes 700
  9.7 41.3 %all-to-all-start = ((f32[128,16,1,256]{3,1,2,0:T(8,128)}), f32[128,16,1,256]{3,1,2,0:T(8,128)S(1)}, u32[]{:S(2)}, u32[]{:S(2)}) async-start(f32[128,16,1,256]{3,1,2,0:T(8,128)} %bitcast.104), calls=%async_computation | async-start | bytes 4194304 | tf_op jit(solution)/shard_map/all_to_all | solution.py:72
  21.2 453.1 %all-gather.3.cloned.1.call-start = ((), (), s32[]{:S(2)}) async-start(), calls=%async_computation.2 | async-start | bytes 24231936 | tf_op jit(solution)/shard_map/all_gather | solution.py:110
  261.7 3.1 copy-start.2
  325.4 10.3 %copy-start.4 = (s32[48,1]{0,1:T(1,128)S(1)}, s32[48,1]{0,1:T(1,128)}, u32[]{:S(2)}) copy-start(s32[48,1]{0,1:T(1,128)} %param.8) | copy-start | bytes 580
  592.8 0.7 copy-start.1
Sparse Core Ops, SparseCore 0:
  335.9 138.4 all-gather.2
where the time goes:
time: 605 us; the launch traced here: 601 us
  local copies, waits for them, and re-layouts  264 us (44%)
  waiting for transfers between devices  163 us (27%)
  matrix products  68.8 us (11%)
  other arithmetic  45.8 us (8%)
  blocking collectives  28 us (5%)
  between operations  13.9 us (2%)
  starting transfers between devices  11.5 us (2%)
    gather x174, local copies, waits for them, and re-layouts  163 us
    all_gather x1, waiting for transfers between devices, body(): piece = lax.all_gather(local[None], 'chan', axis=0, tiled=True)  134 us
    dot_general x1, matrix products, body(): jnp.dot(framed, dft_table(group_freq), precision=lax.Precision.HIGHEST, p...  43.3 us
    all_to_all x1, waiting for transfers between devices, body(): lax.all_to_all(moved, ('tm', 'chan'), split_axis=0, concat_axis=2, tiled=...  29.5 us
    all_to_all x1, blocking collectives, body(): lax.all_to_all(whitened, 'tm', split_axis=2, concat_axis=1, tiled=True)  28 us
    all_gather x1, local copies, waits for them, and re-layouts, body(): piece = lax.all_gather(local[None], 'chan', axis=0, tiled=True)  21.8 us
    select_n x1, other arithmetic, body(): held = jnp.where(inside[:, None, None, None, None], picked, holder)  16.8 us
    gather x1, local copies, waits for them, and re-layouts, body(): picked = piece[jnp.clip(needed, 0, count - 1)]  16.6 us
  transfers between devices with their start and end apart: 2, of which 2 were waited for; matrix products, arithmetic and copies ran while one was open for 1% of the time, Pallas kernels for 0%

commit v1 on v0

v1 whole, which is shorter than its diff:
```python
import functools
import math
import jax
import jax.numpy as jnp
import ml_dtypes
import numpy as np
from jax import lax
from jax.experimental import pallas as pl
from jax.experimental.pallas import tpu as pltpu
from jax.sharding import PartitionSpec as P

NFFT = 1024
NFREQ = 384
WBAND = 64
SEG = 58
SEGP = 64
PMAX = 6
LANES = 128
KROWS = 2 * SEG
QUAD = 4
VMEM_LIMIT = 56 * 1024 * 1024


def windowed_table():
    sample = np.arange(NFFT)
    freq = np.arange(NFREQ)
    angle = 2.0 * np.pi * ((freq[:, None] * sample[None, :]) % NFFT) / NFFT
    window = 0.5 - 0.5 * np.cos(2.0 * np.pi * sample / NFFT)
    table = np.concatenate([np.cos(angle), -np.sin(angle)], axis=0) * window[None, :]
    high = table.astype(np.float32).astype(ml_dtypes.bfloat16)
    low = (table - high.astype(np.float64)).astype(np.float32).astype(ml_dtypes.bfloat16)
    return high, low


def pick_table():
    pick = np.zeros((QUAD * KROWS, QUAD * LANES), np.float32)
    for q in range(QUAD):
        for part in range(2):
            for s in range(SEG):
                pick[q * KROWS + part * SEG + s, q * LANES + part * SEGP + s] = 1.0
    return pick.astype(ml_dtypes.bfloat16)


def slot_table(owners, owner_count):
    owner = owners[:, 0]
    npair = owner.shape[0]
    order = jnp.arange(npair, dtype=jnp.int32)
    same = owner[:, None] == owner[None, :]
    before = order[None, :] < order[:, None]
    rank = jnp.sum((same & before).astype(jnp.int32), axis=1)
    target = owner * PMAX + rank
    rows = jnp.arange(owner_count * PMAX, dtype=jnp.int32)
    match = target[None, :] == rows[:, None]
    live = jnp.any(match, axis=1)
    pair_id = jnp.sum(jnp.where(match, order[None, :], 0), axis=1)
    return (pair_id, live)


def spectra_kernel(chan_count, tm_count, starts_ref, rec_ref, high_ref, low_ref, out_ref, frames, spread):
    sub = rec_ref.shape[1]
    tiles = rec_ref.shape[2] // LANES
    total_tiles = rec_ref.shape[0] * tiles
    width = NFFT // LANES
    lane = lax.broadcasted_iota(jnp.int32, (sub, LANES), 1)
    for c in range(sub):
        frames[:, c * SEGP + SEG : (c + 1) * SEGP, :] = jnp.zeros(
            (width, SEGP - SEG, LANES), jnp.float32
        )

    def cut(s, carry):
        begin = starts_ref[s]
        base = jnp.minimum(begin // LANES, total_tiles - width - 1)
        over = begin - base * LANES
        shift = (LANES - over) % LANES
        turned = []
        for j in range(width + 1):
            tile = base + j
            piece = tile // tiles
            source = (piece % chan_count) * tm_count + piece // chan_count
            at = pl.multiple_of((tile % tiles) * LANES, LANES)
            turned.append(pltpu.roll(rec_ref[source, :, pl.ds(at, LANES)], shift, 1))
        keep = lane < LANES - over
        for j in range(width):
            frames[j, pl.ds(s, sub, stride=SEGP), :] = jnp.where(keep, turned[j], turned[j + 1])
        return carry

    lax.fori_loop(0, SEG, cut, 0)

    group = 4
    cols = group * SEGP
    dims = (((1,), (1,)), ((), ()))
    half = lax.broadcasted_iota(jnp.int32, (NFREQ, LANES), 1) < SEGP

    def transform(g, carry):
        at = pl.ds(pl.multiple_of(g * cols, cols), cols)
        rows = jnp.concatenate([frames[j, at, :] for j in range(width)], axis=1)
        top = rows.astype(jnp.bfloat16)
        rest = (rows - top.astype(jnp.float32)).astype(jnp.bfloat16)
        parts = []
        for p in range(2):
            hi = high_ref[p * NFREQ : (p + 1) * NFREQ, :]
            lo = low_ref[p * NFREQ : (p + 1) * NFREQ, :]
            value = lax.dot_general(hi, rest, dims, preferred_element_type=jnp.float32)
            value += lax.dot_general(lo, top, dims, preferred_element_type=jnp.float32)
            value += lax.dot_general(hi, top, dims, preferred_element_type=jnp.float32)
            parts.append(value)
        re, im = parts
        power = re * re + im * im
        band = jnp.mean(power.reshape(NFREQ // WBAND, WBAND, cols), axis=1, keepdims=True)
        scale = 1.0 / jnp.sqrt(band + 1e-06)
        scale = jnp.broadcast_to(scale, (NFREQ // WBAND, WBAND, cols)).reshape(NFREQ, cols)
        re = re * scale
        im = im * scale
        for h in range(group // 2):
            a = re[:, h * LANES : (h + 1) * LANES]
            b = im[:, h * LANES : (h + 1) * LANES]
            c = g * group + 2 * h
            even = pl.multiple_of(c * NFREQ, NFREQ)
            spread[pl.ds(even, NFREQ), :] = jnp.where(half, a, pltpu.roll(b, SEGP, 1))
            odd = pl.multiple_of((c + 1) * NFREQ, NFREQ)
            spread[pl.ds(odd, NFREQ), :] = jnp.where(half, pltpu.roll(a, SEGP, 1), b)
        return carry

    lax.fori_loop(0, sub // group, transform, 0)

    def regroup(f, carry):
        for u in range(8):
            k = f * 8 + u
            out_ref[k] = spread[pl.ds(k, sub, stride=NFREQ), :].astype(jnp.bfloat16)
        return carry

    lax.fori_loop(0, NFREQ // 8, regroup, 0)


def spectra(starts, received, chan_count, tm_count):
    sub = received.shape[1]
    high, low = windowed_table()
    vmem = pl.BlockSpec(memory_space=pltpu.VMEM)
    return pl.pallas_call(
        functools.partial(spectra_kernel, chan_count, tm_count),
        out_shape=jax.ShapeDtypeStruct((NFREQ, sub, LANES), jnp.bfloat16),
        in_specs=[pl.BlockSpec(memory_space=pltpu.SMEM), vmem, vmem, vmem],
        out_specs=vmem,
        scratch_shapes=[
            pltpu.VMEM((NFFT // LANES, sub * SEGP, LANES), jnp.float32),
            pltpu.VMEM((sub * NFREQ, LANES), jnp.float32),
        ],
        compiler_params=pltpu.CompilerParams(vmem_limit_bytes=VMEM_LIMIT),
    )(starts, received, jnp.asarray(high), jnp.asarray(low))


def compact_kernel(in_ref, pick_ref, out_ref):
    pieces, freqs, sub, _ = in_ref.shape
    block = pieces * sub
    dims = (((1,), (1,)), ((), ()))

    def one(g, carry):
        wide = jnp.concatenate(
            [
                jnp.concatenate([in_ref[p, g * QUAD + q] for p in range(pieces)], axis=0)
                for q in range(QUAD)
            ],
            axis=1,
        )
        value = lax.dot_general(pick_ref[...], wide, dims, preferred_element_type=jnp.float32)
        out_ref[g] = value.astype(jnp.bfloat16)
        return carry

    lax.fori_loop(0, freqs // QUAD, one, 0)


def compact(banded):
    pieces, freqs, sub, _ = banded.shape
    vmem = pl.BlockSpec(memory_space=pltpu.VMEM)
    return pl.pallas_call(
        compact_kernel,
        out_shape=jax.ShapeDtypeStruct((freqs // QUAD, QUAD * KROWS, pieces * sub), jnp.bfloat16),
        in_specs=[vmem, vmem],
        out_specs=vmem,
        compiler_params=pltpu.CompilerParams(vmem_limit_bytes=VMEM_LIMIT),
    )(banded, jnp.asarray(pick_table()))


def product_kernel(needed_ref, live_ref, left_ref, right_ref, out_ref):
    slot = pl.program_id(0)
    quads = left_ref.shape[1]
    block = left_ref.shape[3]
    norm = 1.0 / math.sqrt(SEG)
    dims = (((0,), (0,)), ((), ()))

    @pl.when(live_ref[slot] != 0)
    def _():
        def one(g, carry):
            left4 = left_ref[0, g]
            right4 = right_ref[0, g]
            for q in range(QUAD):
                left = left4[q * KROWS : (q + 1) * KROWS]
                right = right4[q * KROWS : (q + 1) * KROWS]
                turned = jnp.concatenate([-right[SEG:], right[:SEG]], axis=0)
                both = jnp.concatenate([right, turned], axis=1)
                value = lax.dot_general(left, both, dims, preferred_element_type=jnp.float32)
                value = (value * norm).astype(jnp.bfloat16)
                out_ref[0, g * QUAD + q, 0] = value[:, :block]
                out_ref[0, g * QUAD + q, 1] = value[:, block:]
            return carry

        lax.fori_loop(0, quads, one, 0)

    @pl.when(live_ref[slot] == 0)
    def _():
        out_ref[...] = jnp.zeros_like(out_ref)


def products(held, needed, live):
    _, groups, rows, block = held.shape
    step = 4
    freqs = groups * QUAD
    return pl.pallas_call(
        product_kernel,
        out_shape=jax.ShapeDtypeStruct((PMAX, freqs, 2, block, block), jnp.bfloat16),
        grid_spec=pltpu.PrefetchScalarGridSpec(
            num_scalar_prefetch=2,
            grid=(PMAX, groups // step),
            in_specs=[
                pl.BlockSpec((1, step, rows, block), lambda s, g, need, live: (need[2 * s], g, 0, 0)),
                pl.BlockSpec((1, step, rows, block), lambda s, g, need, live: (need[2 * s + 1], g, 0, 0)),
            ],
            out_specs=pl.BlockSpec(
                (1, step * QUAD, 2, block, block), lambda s, g, need, live: (s, g, 0, 0, 0)
            ),
        ),
        compiler_params=pltpu.CompilerParams(vmem_limit_bytes=VMEM_LIMIT),
    )(needed, live, held, held)


def body(records, pairs, owners, starts):
    tm_count = lax.axis_size("tm")
    chan_count = lax.axis_size("chan")
    chans, samp_dev = records.shape
    block = chans // chan_count
    sub = block // tm_count
    group_freq = NFREQ // tm_count
    moved = records.reshape(chan_count * tm_count, sub, samp_dev)
    received = lax.all_to_all(moved, ("chan", "tm"), split_axis=0, concat_axis=0, tiled=True)
    white = spectra(starts, received, chan_count, tm_count)
    white = white.reshape(tm_count, group_freq, sub, LANES)
    banded = lax.all_to_all(white, "tm", split_axis=0, concat_axis=0, tiled=True)
    local = compact(banded)
    held = lax.all_gather(local[None], "chan", axis=0, tiled=True)
    pair_id, live = slot_table(owners, chan_count)
    me_chan = lax.axis_index("chan")
    mine = lax.dynamic_slice_in_dim(pair_id, me_chan * PMAX, PMAX)
    my_live = lax.dynamic_slice_in_dim(live, me_chan * PMAX, PMAX).astype(jnp.int32)
    needed = pairs[mine].reshape(2 * PMAX)
    return products(held, needed, my_live)


def solution(mesh):
    return jax.shard_map(
        body,
        mesh=mesh,
        in_specs=(P(None, ("tm", "chan")), P(), P(), P()),
        out_specs=P("chan", "tm", None, None, None),
        check_vma=False,
    )
```

time: 605 us -> 275 us (0.45)
  local copies, waits for them, and re-layouts: 264 us -> 1.27 us
  matrix products: 68.8 us -> 0 us
  Pallas kernels: 0 us -> 54.6 us
  other arithmetic: 45.8 us -> 1.05 us
  blocking collectives: 28 us -> 68.3 us
  waiting for transfers between devices: 163 us -> 135 us
  starting transfers between devices: 11.5 us -> 0.01 us
    gather x177 -> x1, local copies, waits for them, and re-layouts: 183 us -> 0.56 us  [body(): needed = pairs[mine].reshape(2 * PMAX)]
    dot_general x13 -> x0, matrix products: 68.8 us -> none  [the longest x1 43.3 us: body(): jnp.dot(framed, dft_table(group_freq), precision=lax.Precision.HIGHEST, p...]
    pallas_call x0 -> x3, Pallas kernels: none -> 54.6 us  [the longest x1 24.9 us: products(): pl.pallas_call(product_kernel, out_shape=jax.ShapeDtypeStruct((PMAX, freq...]
    all_to_all x1 -> x2, blocking collectives: 28 us -> 68.3 us  [the longest x1 42.1 us: body(): lax.all_to_all(moved, ('chan', 'tm'), split_axis=0, concat_axis=0, tiled=...]
    all_to_all x1 -> x0, waiting for transfers between devices: 29.5 us -> none  [body(): lax.all_to_all(moved, ('tm', 'chan'), split_axis=0, concat_axis=2, tiled=...]
    all_gather x1 -> x0, local copies, waits for them, and re-layouts: 21.8 us -> none  [body(): piece = lax.all_gather(local[None], 'chan', axis=0, tiled=True)]
    reshape x4 -> x1, local copies, waits for them, and re-layouts: 18.4 us -> 0.62 us  [body(): needed = pairs[mine].reshape(2 * PMAX)]
    select_n x2 -> x1, other arithmetic: 16.8 us -> 0.08 us  [body(): needed = pairs[mine].reshape(2 * PMAX)]
  transfers between devices with their start and end apart: 2 -> 1, of which waited for: 2 -> 1; matrix products, arithmetic and copies ran while one was open for 1% -> 1% of each run, Pallas kernels for 0% -> 0%
where the time goes in v1:
time: 275 us; the launch traced here: 274 us
  waiting for transfers between devices  135 us (49%)
  blocking collectives  68.3 us (25%)
  Pallas kernels  54.6 us (20%)
  between operations  13.4 us (5%)
    all_gather x1, waiting for transfers between devices, body(): held = lax.all_gather(local[None], 'chan', axis=0, tiled=True)  135 us
    all_to_all x1, blocking collectives, body(): lax.all_to_all(moved, ('chan', 'tm'), split_axis=0, concat_axis=0, tiled=...  42.1 us
    all_to_all x1, blocking collectives, body(): lax.all_to_all(white, 'tm', split_axis=0, concat_axis=0, tiled=True)  26.2 us
    pallas_call x1, Pallas kernels, products(): pl.pallas_call(product_kernel, out_shape=jax.ShapeDtypeStruct((PMAX, freq...  24.9 us
    pallas_call x1, Pallas kernels, spectra(): pl.pallas_call(functools.partial(spectra_kernel, chan_count, tm_count), o...  23.7 us
    pallas_call x1, Pallas kernels, compact(): pl.pallas_call(compact_kernel, out_shape=jax.ShapeDtypeStruct((freqs // Q...  6 us
  transfers between devices with their start and end apart: 1, of which 1 were waited for; matrix products, arithmetic and copies ran while one was open for 1% of the time, Pallas kernels for 0%

profile of v1, /device:TPU:1, one launch (start us, length us, event | category | flops | bytes accessed | tf_op | source)
XLA Modules:
  0.0 274.0 jit_solution(14342756503969865348)
XLA Ops:
  6.5 0.0 all-gather.3.cloned.1.call-start
  6.5 42.1 %all_to_all.10.rec_ref = f32[128,16,256]{2,1,0:T(8,128)} all-to-all(f32[128,16,256]{2,1,0:T(8,128)} %bitcast.8), channel_id=1, replica_groups=mesh['tm'=8,'chan'=16] {'chan','tm'}, dimensions={0} | all-to-all | bytes 4194304 | tf_op jit(solution)/shard_map/all_to_all | solution.py:244
  48.7 23.7 %shard_map.73 = bf16[384,16,128]{2,1,0:T(8,128)(2,1)} custom-call(s32[58]{0:T(128)} %starts_ref.1, f32[128,16,256]{2,1,0:T(8,128)} %all_to_all.10.rec_ref, bf16[768,1024]{1,0:T(8,128)(2,1)} %constant.7.clone.high_ref, bf16[768,1024]{1,0:T(8,128)(2,1)} %constant.8.clone.low_ref), custom_call_target="tpu_custom_call" | custom-call | tf_op jit(solution)/shard_map/pallas_call | solution.py:139
  72.4 26.2 %all_to_all.11.in_ref = bf16[8,48,16,128]{3,2,1,0:T(8,128)(2,1)} all-to-all(bf16[8,48,16,128]{3,2,1,0:T(8,128)(2,1)} %bitcast.7), channel_id=1, replica_groups=mesh['tm'=8,'chan'=16] {'tm'}, dimensions={0} | all-to-all | bytes 3145728 | tf_op jit(solution)/shard_map/all_to_all | solution.py:247
  98.6 0.0 copy-start
  98.6 0.0 copy-start.1
  98.6 6.0 %shard_map.74 = bf16[12,464,128]{2,1,0:T(8,128)(2,1)} custom-call(bf16[8,48,16,128]{3,2,1,0:T(8,128)(2,1)} %all_to_all.11.in_ref, bf16[464,512]{1,0:T(8,128)(2,1)} %constant.24.clone.pick_ref), custom_call_target="tpu_custom_call" | custom-call | tf_op jit(solution)/shard_map/pallas_call | solution.py:175
  104.6 0.0 all-gather.3.cloned.1.call-update
  104.6 0.0 copy-done
  104.7 0.1 copy.11
  104.7 0.0 copy-done.1
  104.7 0.2 convert_reduce_fusion
  104.9 0.1 select_reduce_fusion
  105.0 0.1 compare_select_fusion
  105.1 0.6 gather_fusion
  105.7 0.6 reshape.18.needed_ref
  106.3 0.1 fusion
  106.4 0.6 dynamic-slice_convert_fusion.live_ref
  107.0 135.3 %all-gather.3.cloned.1.call-done = bf16[192,464,128]{2,1,0:T(8,128)(2,1)} async-done(((bf16[12,464,128]{2,1,0:T(8,128)(2,1)}), bf16[192,464,128]{2,1,0:T(8,128)(2,1)}) %all-gather.3.cloned.1.call-update) | async-done | bytes 22806544 | tf_op jit(solution)/shard_map/all_gather | solution.py:249
  242.3 24.9 %shard_map.75 = bf16[6,48,2,128,128]{4,3,2,1,0:T(8,128)(2,1)} custom-call(s32[12]{0:T(128)} %reshape.18.needed_ref, s32[6]{0:T(128)} %dynamic-slice_convert_fusion.live_ref, bf16[16,12,464,128]{3,2,1,0:T(8,128)(2,1)} %bitcast.5, bf16[16,12,464,128]{3,2,1,0:T(8,128)(2,1)} %bitcast.6), custom_call_target="tpu_custom_call" | custom-call | tf_op jit(solution)/shard_map/pallas_call | solution.py:218
  (2 shorter events, 0.0 us)
Async XLA Ops:
  6.5 235.7 %all-gather.3.cloned.1.call-start = ((), (), s32[]{:S(2)}) async-start(), calls=%async_computation.2 | async-start | bytes 24231936 | tf_op jit(solution)/shard_map/all_gather | solution.py:249
  98.6 6.0 %copy-start = (s32[48,2]{0,1:T(2,128)S(1)}, s32[48,2]{0,1:T(2,128)}, u32[]{:S(2)}) copy-start(s32[48,2]{0,1:T(2,128)} %param.8) | copy-start | bytes 1156
  98.6 6.1 %copy-start.1 = (s32[48,1]{0,1:T(1,128)S(1)}, s32[48,1]{0,1:T(1,128)}, u32[]{:S(2)}) copy-start(s32[48,1]{0,1:T(1,128)} %param.9) | copy-start | bytes 580
Sparse Core Ops, SparseCore 0:
  104.8 137.4 all-gather.2

commit v2 on v1

--- a/solution.py
+++ b/solution.py
@@ -19,6 +19,10 @@
 KROWS = 2 * SEG
 QUAD = 4
 VMEM_LIMIT = 56 * 1024 * 1024
+THIRDS = 3
+STREAMS = 2
+MAX_ROUNDS = 32
+ROUND_CHOICES = (7, 8, 9)
 
 
 def windowed_table():
@@ -181,18 +185,255 @@
     )(banded, jnp.asarray(pick_table()))
 
 
+def torus_tables(count):
+    side = math.isqrt(count)
+    index = np.arange(count)
+    x, y = index // side, index % side
+    sources = [
+        (x + 1) % side * side + y,
+        (x - 1) % side * side + y,
+        x * side + (y + 1) % side,
+        x * side + (y - 1) % side,
+    ]
+    near = np.concatenate([np.eye(count)[source] for source in sources], axis=0)
+    dx = np.abs(x[:, None] - x[None, :])
+    dy = np.abs(y[:, None] - y[None, :])
+    dist = np.minimum(dx, side - dx) + np.minimum(dy, side - dy)
+    reach = np.concatenate([dist <= d for d in range(4)], axis=0)
+    shell = np.concatenate([(dist == d) * 2.0 ** (3 - d) for d in range(4)], axis=1)
+    return [t.astype(ml_dtypes.bfloat16) for t in (near, reach, shell)]
+
+
+def plan_kernel(pairs_ref, owners_ref, near_ref, reach_ref, shell_ref, table_ref, slots_ref, rounds_ref):
+    count = near_ref.shape[1]
+    shape = (count, LANES)
+    node = lax.broadcasted_iota(jnp.int32, shape, 0)
+    lane = lax.broadcasted_iota(jnp.int32, shape, 1)
+    inside = lane < THIRDS * count
+    block = lane % count
+    third = lane // count
+    commodities = THIRDS * count
+    tie = commodities - 1 - (lane + 3 * node) % commodities
+    tie = jnp.where(inside, tie, 0).astype(jnp.float32)
+
+    def mark(p, need):
+        hit = (block == pairs_ref[p, 0]) | (block == pairs_ref[p, 1])
+        return jnp.where(hit & (node == owners_ref[p, 0]) & inside, 1.0, need)
+
+    need = lax.fori_loop(0, pairs_ref.shape[0], mark, jnp.zeros(shape, jnp.float32))
+    has = jnp.where((block == node) & inside, 1.0, 0.0)
+    slot_of = jnp.where(has > 0, third, 0).astype(jnp.float32)
+    table = jnp.zeros(shape, jnp.float32)
+
+    def dot(m, v):
+        return jnp.dot(m, v.astype(jnp.bfloat16), preferred_element_type=jnp.float32)
+
+    def unfinished(state):
+        r, left, _, _, _ = state
+        return (left > 0) & (r < MAX_ROUNDS)
+
+    def one(state):
+        r, _, has, slot_of, table = state
+        rem = need * (1.0 - has)
+        short = rem * jnp.sum(rem, axis=1, keepdims=True)
+        reached = dot(reach_ref[...], has)
+        waves = jnp.concatenate(
+            [jnp.where(reached[d * count : (d + 1) * count] > 0, 0.0, short) for d in range(4)], axis=0
+        )
+        gain = dot(shell_ref[...], waves)
+        both = dot(near_ref[...], jnp.concatenate([has, slot_of], axis=1))
+        near_has = [both[k * count : (k + 1) * count, :LANES] for k in range(4)]
+        near_slot = [both[k * count : (k + 1) * count, LANES:] for k in range(4)]
+        sources = near_has[0] + near_has[1] + near_has[2] + near_has[3]
+        worth = jnp.where((gain > 0) & (has == 0), gain * (5.0 - sources) * 64.0 + tie, 0.0)
+        for k in range(4):
+            key = worth * near_has[k]
+            best = jnp.max(key, axis=1, keepdims=True)
+            chosen = (key == best) & (key > 0)
+            worth = jnp.where(chosen, 0.0, worth)
+            has = jnp.where(chosen, 1.0, has)
+            source = jnp.sum(jnp.where(chosen, near_slot[k], 0.0), axis=1, keepdims=True)
+            table = jnp.where(lane == 4 * r + k, source, table)
+            slot_of = jnp.where(chosen, (THIRDS + 4 * r + k).astype(jnp.float32), slot_of)
+        left = jnp.sum(need * (1.0 - has))
+        return r + 1, left, has, slot_of, table
+
+    left = jnp.sum(need * (1.0 - has))
+    rounds, left, has, slot_of, table = lax.while_loop(
+        unfinished, one, (jnp.int32(0), left, has, slot_of, table)
+    )
+    table_ref[...] = table.astype(jnp.int32)
+    slots_ref[...] = slot_of.astype(jnp.int32)
+    rounds_ref[...] = jnp.full(rounds_ref.shape, jnp.where(left > 0, MAX_ROUNDS, rounds), jnp.int32)
+
+
+def plan(pairs, owners, count):
+    near, reach, shell = torus_tables(count)
+    vmem = pl.BlockSpec(memory_space=pltpu.VMEM)
+    smem = pl.BlockSpec(memory_space=pltpu.SMEM)
+    grid = jax.ShapeDtypeStruct((count, LANES), jnp.int32)
+    return pl.pallas_call(
+        plan_kernel,
+        out_shape=(grid, grid, jax.ShapeDtypeStruct((8, LANES), jnp.int32)),
+        in_specs=[smem, smem, vmem, vmem, vmem],
+        out_specs=(vmem, vmem, vmem),
+    )(pairs, owners, jnp.asarray(near), jnp.asarray(reach), jnp.asarray(shell))
+
+
+def exchange_kernel(count, rounds, table_ref, own_ref, out_ref, held, land, stage, send_sem, recv_sem, out_sem):
+    side = math.isqrt(count)
+    me = lax.axis_index("chan")
+    x, y = me // side, me % side
+    targets = [
+        (x + side - 1) % side * side + y,
+        (x + 1) % side * side + y,
+        x * side + (y + side - 1) % side,
+        x * side + (y + 1) % side,
+    ]
+    rows = own_ref.shape[2]
+    step = 32
+
+    barrier = pltpu.get_barrier_semaphore()
+    for k in range(4):
+        pl.semaphore_signal(
+            barrier, inc=1, device_id={"chan": targets[k]}, device_id_type=pl.DeviceIdType.MESH
+        )
+    pl.semaphore_wait(barrier, 4)
+
+    def each_chunk(work):
+        def run(i, carry):
+            work(pl.ds(pl.multiple_of(i * step, step), step))
+            return carry
+
+        lax.fori_loop(0, rows // step, run, 0)
+
+    def remote(parity, h, k):
+        return pltpu.make_async_remote_copy(
+            src_ref=stage.at[parity, h, k],
+            dst_ref=land.at[parity, h, k],
+            send_sem=send_sem.at[parity, h, k],
+            recv_sem=recv_sem.at[parity, h, k],
+            device_id={"chan": targets[k]},
+            device_id_type=pl.DeviceIdType.MESH,
+        )
+
+    def keep_own(h):
+        return pltpu.make_async_copy(
+            own_ref.at[:, h], out_ref.at[pl.ds(0, THIRDS), h], out_sem.at[rounds, h]
+        )
+
+    def keep(r, h):
+        at = pl.ds(THIRDS + 4 * r, 4)
+        return pltpu.make_async_copy(held.at[at, h], out_ref.at[at, h], out_sem.at[r, h])
+
+    def absorb(r, h):
+        parity = r % 2
+        for k in range(4):
+            remote(parity, h, k).wait_recv()
+
+        def work(at):
+            for k in range(4):
+                held[THIRDS + 4 * r + k, h, at, :] = land[parity, h, k, at, :]
+
+        each_chunk(work)
+        keep(r, h).start()
+
+    def send(r, h):
+        parity = r % 2
+        source = [table_ref[targets[k], 4 * r + k] for k in range(4)]
+
+        def work(at):
+            for k in range(4):
+                stage[parity, h, k, at, :] = held[source[k], h, at, :]
+
+        each_chunk(work)
+        for k in range(4):
+            remote(parity, h, k).start()
+
+    for h in range(STREAMS):
+
+        def work(at):
+            for s in range(THIRDS):
+                held[s, h, at, :] = own_ref[s, h, at, :]
+
+        each_chunk(work)
+        send(0, h)
+        keep_own(h).start()
+    for h in range(STREAMS):
+        absorb(0, h)
+        send(1, h)
+
+    def general(r, carry):
+        for h in range(STREAMS):
+            absorb(r - 1, h)
+            for k in range(4):
+                remote(r % 2, h, k).wait_send()
+            send(r, h)
+        return carry
+
+    lax.fori_loop(2, rounds, general, 0)
+    for h in range(STREAMS):
+        absorb(rounds - 1, h)
+        for parity in range(2):
+            for k in range(4):
+                remote(parity, h, k).wait_send()
+    for h in range(STREAMS):
+        keep_own(h).wait()
+        for r in range(rounds):
+            keep(r, h).wait()
+
+
+def exchange(table, own, count, rounds, ident):
+    _, streams, rows, block = own.shape
+    return pl.pallas_call(
+        functools.partial(exchange_kernel, count, rounds),
+        out_shape=jax.ShapeDtypeStruct((THIRDS * count, streams, rows, block), own.dtype),
+        in_specs=[pl.BlockSpec(memory_space=pltpu.SMEM), pl.BlockSpec(memory_space=pltpu.VMEM)],
+        out_specs=pl.BlockSpec(memory_space=pl.ANY),
+        scratch_shapes=[
+            pltpu.VMEM((THIRDS + 4 * rounds, streams, rows, block), own.dtype),
+            pltpu.VMEM((2, streams, 4, rows, block), own.dtype),
+            pltpu.VMEM((2, streams, 4, rows, block), own.dtype),
+            pltpu.SemaphoreType.DMA((2, streams, 4)),
+            pltpu.SemaphoreType.DMA((2, streams, 4)),
+            pltpu.SemaphoreType.DMA((rounds + 1, streams)),
+        ],
+        compiler_params=pltpu.CompilerParams(
+            vmem_limit_bytes=VMEM_LIMIT, collective_id=ident, has_side_effects=True
+        ),
+    )(table, own)
+
+
+def gather_needed(table, slots, rounds, own, me, count):
+    mine = lax.dynamic_index_in_dim(slots, me, 0, keepdims=False)
+    every = np.arange(LANES)
+    every = np.where(every < THIRDS * count, every % count * THIRDS + every // count, 0)
+    every = jnp.asarray(every, jnp.int32)
+
+    def by_rounds(choice, ident):
+        return lambda: (exchange(table, own, count, choice, ident), mine)
+
+    def whole():
+        return lax.all_gather(own, "chan", axis=0, tiled=True), every
+
+    branches = [by_rounds(choice, i) for i, choice in enumerate(ROUND_CHOICES)] + [whole]
+    which = sum((rounds > choice).astype(jnp.int32) for choice in ROUND_CHOICES)
+    return lax.switch(which, branches)
+
+
 def product_kernel(needed_ref, live_ref, left_ref, right_ref, out_ref):
     slot = pl.program_id(0)
-    quads = left_ref.shape[1]
-    block = left_ref.shape[3]
+    streams, rows, block = left_ref.shape[1:]
     norm = 1.0 / math.sqrt(SEG)
     dims = (((0,), (0,)), ((), ()))
+    per = rows // (QUAD * KROWS)
 
     @pl.when(live_ref[slot] != 0)
     def _():
         def one(g, carry):
-            left4 = left_ref[0, g]
-            right4 = right_ref[0, g]
+            at = pl.ds(pl.multiple_of(g % per * (QUAD * KROWS), 16), QUAD * KROWS)
+            left4 = left_ref[0, g // per, at]
+            right4 = right_ref[0, g // per, at]
             for q in range(QUAD):
                 left = left4[q * KROWS : (q + 1) * KROWS]
                 right = right4[q * KROWS : (q + 1) * KROWS]
@@ -204,7 +445,7 @@
                 out_ref[0, g * QUAD + q, 1] = value[:, block:]
             return carry
 
-        lax.fori_loop(0, quads, one, 0)
+        lax.fori_loop(0, streams * per, one, 0)
 
     @pl.when(live_ref[slot] == 0)
     def _():
@@ -212,22 +453,20 @@
 
 
 def products(held, needed, live):
-    _, groups, rows, block = held.shape
-    step = 4
-    freqs = groups * QUAD
+    _, streams, rows, block = held.shape
+    part = streams * rows // KROWS
+    spec = (1, streams, rows, block)
     return pl.pallas_call(
         product_kernel,
-        out_shape=jax.ShapeDtypeStruct((PMAX, freqs, 2, block, block), jnp.bfloat16),
+        out_shape=jax.ShapeDtypeStruct((PMAX, THIRDS * part, 2, block, block), jnp.bfloat16),
         grid_spec=pltpu.PrefetchScalarGridSpec(
             num_scalar_prefetch=2,
-            grid=(PMAX, groups // step),
+            grid=(PMAX, THIRDS),
             in_specs=[
-                pl.BlockSpec((1, step, rows, block), lambda s, g, need, live: (need[2 * s], g, 0, 0)),
-                pl.BlockSpec((1, step, rows, block), lambda s, g, need, live: (need[2 * s + 1], g, 0, 0)),
+                pl.BlockSpec(spec, lambda s, g, need, live: (need[2 * s, g], 0, 0, 0)),
+                pl.BlockSpec(spec, lambda s, g, need, live: (need[2 * s + 1, g], 0, 0, 0)),
             ],
-            out_specs=pl.BlockSpec(
-                (1, step * QUAD, 2, block, block), lambda s, g, need, live: (s, g, 0, 0, 0)
-            ),
+            out_specs=pl.BlockSpec((1, part, 2, block, block), lambda s, g, need, live: (s, g, 0, 0, 0)),
         ),
         compiler_params=pltpu.CompilerParams(vmem_limit_bytes=VMEM_LIMIT),
     )(needed, live, held, held)
@@ -240,18 +479,20 @@
     block = chans // chan_count
     sub = block // tm_count
     group_freq = NFREQ // tm_count
+    table, slots, rounds = plan(pairs, owners, chan_count)
     moved = records.reshape(chan_count * tm_count, sub, samp_dev)
     received = lax.all_to_all(moved, ("chan", "tm"), split_axis=0, concat_axis=0, tiled=True)
     white = spectra(starts, received, chan_count, tm_count)
     white = white.reshape(tm_count, group_freq, sub, LANES)
     banded = lax.all_to_all(white, "tm", split_axis=0, concat_axis=0, tiled=True)
-    local = compact(banded)
-    held = lax.all_gather(local[None], "chan", axis=0, tiled=True)
+    own = compact(banded).reshape(THIRDS, STREAMS, -1, block)
+    me_chan = lax.axis_index("chan")
+    held, slot_of = gather_needed(table, slots, rounds[0, 0], own, me_chan, chan_count)
     pair_id, live = slot_table(owners, chan_count)
-    me_chan = lax.axis_index("chan")
     mine = lax.dynamic_slice_in_dim(pair_id, me_chan * PMAX, PMAX)
     my_live = lax.dynamic_slice_in_dim(live, me_chan * PMAX, PMAX).astype(jnp.int32)
-    needed = pairs[mine].reshape(2 * PMAX)
+    blocks = pairs[mine].reshape(2 * PMAX)
+    needed = slot_of[blocks[:, None] + chan_count * jnp.arange(THIRDS, dtype=jnp.int32)[None, :]]
     return products(held, needed, my_live)
 
 

time: 275 us -> 217 us (0.79)
  waiting for transfers between devices: 135 us -> 7.62 us
  Pallas kernels: 54.6 us -> 140 us
  blocking collectives: 68.3 us -> 42.1 us
  starting transfers between devices: 0.01 us -> 4.78 us
  local copies, waits for them, and re-layouts: 1.27 us -> 5.3 us
    all_gather x1 -> x0, waiting for transfers between devices: 135 us -> none  [body(): held = lax.all_gather(local[None], 'chan', axis=0, tiled=True)]
    pallas_call x1 -> x3, Pallas kernels: 24.9 us -> 111 us  [the longest x1 76.6 us: exchange(): pl.pallas_call(functools.partial(exchange_kernel, count, rounds), out_sha...]
    all_to_all x1 -> x0, blocking collectives: 26.2 us -> none  [body(): lax.all_to_all(white, 'tm', split_axis=0, concat_axis=0, tiled=True)]
    all_to_all x0 -> x1, waiting for transfers between devices: none -> 7.62 us  [body(): lax.all_to_all(white, 'tm', split_axis=0, concat_axis=0, tiled=True)]
    all_to_all x0 -> x1, starting transfers between devices: none -> 4.78 us  [body(): lax.all_to_all(white, 'tm', split_axis=0, concat_axis=0, tiled=True)]
  transfers between devices with their start and end apart: 1 -> 1, of which waited for: 1 -> 1; matrix products, arithmetic and copies ran while one was open for 1% -> 2% of each run, Pallas kernels for 0% -> 3%
where the time goes in v2:
time: 217 us; the launch traced here: 216 us
  Pallas kernels  140 us (65%)
  blocking collectives  42.1 us (19%)
  between operations  15.1 us (7%)
  waiting for transfers between devices  7.62 us (4%)
  local copies, waits for them, and re-layouts  5.3 us (2%)
  starting transfers between devices  4.78 us (2%)
    pallas_call x1, Pallas kernels, exchange(): pl.pallas_call(functools.partial(exchange_kernel, count, rounds), out_sha...  76.6 us
    all_to_all x1, blocking collectives, body(): lax.all_to_all(moved, ('chan', 'tm'), split_axis=0, concat_axis=0, tiled=...  42.1 us
    pallas_call x1, Pallas kernels, products(): pl.pallas_call(product_kernel, out_shape=jax.ShapeDtypeStruct((PMAX, THIR...  26.9 us
    pallas_call x1, Pallas kernels, spectra(): pl.pallas_call(functools.partial(spectra_kernel, chan_count, tm_count), o...  23.7 us
    all_to_all x1, waiting for transfers between devices, body(): lax.all_to_all(white, 'tm', split_axis=0, concat_axis=0, tiled=True)  7.62 us
    pallas_call x1, Pallas kernels, plan(): pl.pallas_call(plan_kernel, out_shape=(grid, grid, jax.ShapeDtypeStruct((...  7.51 us
    pallas_call x1, Pallas kernels, compact(): pl.pallas_call(compact_kernel, out_shape=jax.ShapeDtypeStruct((freqs // Q...  4.88 us
    all_to_all x1, starting transfers between devices, body(): lax.all_to_all(white, 'tm', split_axis=0, concat_axis=0, tiled=True)  4.78 us
  transfers between devices with their start and end apart: 1, of which 1 were waited for; matrix products, arithmetic and copies ran while one was open for 2% of the time, Pallas kernels for 3%

profile of v2, /device:TPU:1, one launch (start us, length us, event | category | flops | bytes accessed | tf_op | source)
XLA Modules:
  0.0 215.8 jit_solution(15755704906644689944)
XLA Ops:
  6.5 42.1 %all_to_all.10.rec_ref = f32[128,16,256]{2,1,0:T(8,128)} all-to-all(f32[128,16,256]{2,1,0:T(8,128)} %bitcast.19), channel_id=1, replica_groups=mesh['tm'=8,'chan'=16] {'chan','tm'}, dimensions={0} | all-to-all | bytes 4194304 | tf_op jit(solution)/shard_map/all_to_all | solution.py:484
  48.7 23.7 %shard_map.111 = bf16[384,16,128]{2,1,0:T(8,128)(2,1)} custom-call(s32[58]{0:T(128)} %starts_ref.1, f32[128,16,256]{2,1,0:T(8,128)} %all_to_all.10.rec_ref, bf16[768,1024]{1,0:T(8,128)(2,1)} %constant.65.clone.high_ref, bf16[768,1024]{1,0:T(8,128)(2,1)} %constant.66.clone.low_ref), custom_call_target="tpu_custom_call" | custom-call | tf_op jit(solution)/shard_map/pallas_call | solution.py:143
  72.4 0.0 copy-start.3
  72.4 0.0 copy-start.4
  72.4 4.8 %all-to-all-start.1 = ((bf16[8,48,16,128]{3,2,1,0:T(8,128)(2,1)}), bf16[8,48,16,128]{3,2,1,0:T(8,128)(2,1)S(1)}, u32[]{:S(2)}, u32[]{:S(2)}) async-start(bf16[8,48,16,128]{3,2,1,0:T(8,128)(2,1)} %bitcast.18), calls=%async_computation.1 | async-start | bytes 3145728 | tf_op jit(solution)/shard_map/all_to_all | solution.py:487
  77.2 0.0 copy-done.3
  77.2 0.1 copy.22.pairs_ref
  77.3 0.0 copy-done.4
  77.3 0.0 copy-start.2
  77.3 0.7 copy.23.owners_ref
  78.0 0.2 convert_reduce_fusion
  78.2 0.1 select_reduce_fusion
  78.3 0.1 compare_select_fusion.1
  78.3 0.6 gather_fusion
  78.9 0.1 add.76
  79.0 0.1 compare_select_fusion
  79.1 0.1 reshape.106
  79.2 0.0 copy-done.2
  79.2 7.5 %shard_map.110 = (s32[16,128]{1,0:T(8,128)S(1)}, s32[16,128]{1,0:T(8,128)S(1)}, s32[8,128]{1,0:T(8,128)}) custom-call(s32[48,2]{1,0:T(8,128)} %copy-done.2, s32[48,1]{1,0:T(8,128)} %copy.23.owners_ref, bf16[64,16]{1,0:T(8,128)(2,1)} %constant.62.clone.near_ref, bf16[64,16]{1,0:T(8,128)(2,1)} %constant.63.clone.reach_ref, bf16[16,64]{1,0:T(8,128)(2,1)} %constant.64.clone.shell_ref), custom_call_target="tpu_custom_call" | custom-call | tf_op jit(solution)/shard_map/pallas_call | solution.py:275
  86.7 1.2 slice.3
  89.5 0.1 fusion
  89.6 0.7 dynamic-slice_convert_fusion.live_ref
  90.3 7.6 %all-to-all-done.1.in_ref = bf16[8,48,16,128]{3,2,1,0:T(8,128)(2,1)S(1)} async-done(((bf16[8,48,16,128]{3,2,1,0:T(8,128)(2,1)}), bf16[8,48,16,128]{3,2,1,0:T(8,128)(2,1)S(1)}, u32[]{:S(2)}, u32[]{:S(2)}) %all-to-all-start.1) | async-done | bytes 1572896 | tf_op jit(solution)/shard_map/all_to_all | solution.py:487
  97.9 0.0 copy-start.1
  97.9 1.1 copy-done.1
  99.1 4.9 %shard_map.112 = bf16[12,464,128]{2,1,0:T(8,128)(2,1)S(1)} custom-call(bf16[8,48,16,128]{3,2,1,0:T(8,128)(2,1)} %copy-done.1, bf16[464,512]{1,0:T(8,128)(2,1)} %constant.67.clone.pick_ref), custom_call_target="tpu_custom_call" | custom-call | tf_op jit(solution)/shard_map/pallas_call | solution.py:179
  104.0 76.7 %conditional.1 = (bf16[48,2,928,128]{3,2,1,0:T(8,128)(2,1)}, s32[128]{0:T(128)S(1)}) conditional(s32[]{:T(128)} %bitcast.3, (s32[16,128]{1,0:T(8,128)S(1)}, bf16[3,2,928,128]{3,2,1,0:T(8,128)(2,1)S(1)}, s32[]{:T(128)}, s32[16,128]{1,0:T(8,128)S(1)}) %tuple.30, (s32[16,128]{1,0:T(8,128)S(1)}, ...), branch_computations={%region_0.1_spmd, %region_1.2_spmd, %region_2.3_spmd, %region_3.4_... | conditional | flops 3 | bytes 78398544 | solution.py:421
  104.0 76.6 %branch_0_fun.1 = bf16[48,2,928,128]{3,2,1,0:T(8,128)(2,1)} custom-call(s32[16,128]{1,0:T(8,128)S(1)} %get-tuple-element.63.table_ref, bf16[3,2,928,128]{3,2,1,0:T(8,128)(2,1)S(1)} %get-tuple-element.64.own_ref), custom_call_target="tpu_custom_call" | custom-call | tf_op jit(solution)/shard_map/cond/branch_0_fun/pallas_call | solution.py:388
  180.6 0.8 gather_fusion.1
  181.4 0.7 reshape.105.needed_ref
  182.1 26.9 %shard_map.113 = bf16[6,48,2,128,128]{4,3,2,1,0:T(8,128)(2,1)} custom-call(s32[12,3]{1,0:T(8,128)} %reshape.105.needed_ref, s32[6]{0:T(128)} %dynamic-slice_convert_fusion.live_ref, bf16[48,2,928,128]{3,2,1,0:T(8,128)(2,1)} %get-tuple-element.86.left_ref.right_ref, bf16[48,2,928,128]{3,2,1,0:T(8,128)(2,1)} %get-tuple-element.86.left_ref.right_ref), custom_call_target="tpu_custom_call" | custom-call | tf_op jit(solution)/shard_map/pallas_call | solution.py:459
  (5 shorter events, 0.0 us)
Async XLA Ops:
  72.4 4.8 %copy-start.3 = (s32[48,2]{0,1:T(2,128)S(1)}, s32[48,2]{0,1:T(2,128)}, u32[]{:S(2)}) copy-start(s32[48,2]{0,1:T(2,128)} %param.16) | copy-start | bytes 1156
  72.4 4.9 %copy-start.4 = (s32[48,1]{0,1:T(1,128)S(1)}, s32[48,1]{0,1:T(1,128)}, u32[]{:S(2)}) copy-start(s32[48,1]{0,1:T(1,128)} %param.17) | copy-start | bytes 580
  72.4 25.5 %all-to-all-start.1 = ((bf16[8,48,16,128]{3,2,1,0:T(8,128)(2,1)}), bf16[8,48,16,128]{3,2,1,0:T(8,128)(2,1)S(1)}, u32[]{:S(2)}, u32[]{:S(2)}) async-start(bf16[8,48,16,128]{3,2,1,0:T(8,128)(2,1)} %bitcast.18), calls=%async_computation.1 | async-start | bytes 3145728 | tf_op jit(solution)/shard_map/all_to_all | solution.py:487
  77.3 1.9 copy-start.2
  97.9 1.1 copy-start.1

commit v3 on v2

--- a/solution.py
+++ b/solution.py
@@ -19,10 +19,13 @@
 KROWS = 2 * SEG
 QUAD = 4
 VMEM_LIMIT = 56 * 1024 * 1024
+EXCHANGE_LIMIT = 28 * 1024 * 1024
+PRODUCT_LIMIT = 12 * 1024 * 1024
 THIRDS = 3
 STREAMS = 2
 MAX_ROUNDS = 32
-ROUND_CHOICES = (7, 8, 9)
+ROUND_CHOICES = (7, 8)
+SCALE = 8192.0
 
 
 def windowed_table():
@@ -30,7 +33,7 @@
     freq = np.arange(NFREQ)
     angle = 2.0 * np.pi * ((freq[:, None] * sample[None, :]) % NFFT) / NFFT
     window = 0.5 - 0.5 * np.cos(2.0 * np.pi * sample / NFFT)
-    table = np.concatenate([np.cos(angle), -np.sin(angle)], axis=0) * window[None, :]
+    table = np.concatenate([np.cos(angle), -np.sin(angle)], axis=0) * window[None, :] / SCALE
     high = table.astype(np.float32).astype(ml_dtypes.bfloat16)
     low = (table - high.astype(np.float64)).astype(np.float32).astype(ml_dtypes.bfloat16)
     return high, low
@@ -60,7 +63,20 @@
     return (pair_id, live)
 
 
-def spectra_kernel(chan_count, tm_count, starts_ref, rec_ref, high_ref, low_ref, out_ref, frames, spread):
+def bits(size):
+    assert size & (size - 1) == 0
+    return size.bit_length() - 1
+
+
+def spectra_kernel(
+    chan_count, tm_count, starts_ref, rec_ref, high_hbm, low_hbm, out_ref, high_ref, low_ref, frames, spread, sems
+):
+    fetch = [
+        pltpu.make_async_copy(high_hbm, high_ref, sems.at[0]),
+        pltpu.make_async_copy(low_hbm, low_ref, sems.at[1]),
+    ]
+    for copy in fetch:
+        copy.start()
     sub = rec_ref.shape[1]
     tiles = rec_ref.shape[2] // LANES
     total_tiles = rec_ref.shape[0] * tiles
@@ -73,22 +89,24 @@
 
     def cut(s, carry):
         begin = starts_ref[s]
-        base = jnp.minimum(begin // LANES, total_tiles - width - 1)
+        base = jnp.minimum(begin >> bits(LANES), total_tiles - width - 1)
         over = begin - base * LANES
-        shift = (LANES - over) % LANES
+        shift = (LANES - over) & (LANES - 1)
         turned = []
         for j in range(width + 1):
             tile = base + j
-            piece = tile // tiles
-            source = (piece % chan_count) * tm_count + piece // chan_count
-            at = pl.multiple_of((tile % tiles) * LANES, LANES)
+            piece = tile >> bits(tiles)
+            source = (piece & (chan_count - 1)) * tm_count + (piece >> bits(chan_count))
+            at = pl.multiple_of((tile & (tiles - 1)) * LANES, LANES)
             turned.append(pltpu.roll(rec_ref[source, :, pl.ds(at, LANES)], shift, 1))
         keep = lane < LANES - over
         for j in range(width):
             frames[j, pl.ds(s, sub, stride=SEGP), :] = jnp.where(keep, turned[j], turned[j + 1])
         return carry
 
-    lax.fori_loop(0, SEG, cut, 0)
+    lax.fori_loop(0, SEG, cut, 0, unroll=2)
+    for copy in fetch:
+        copy.wait()
 
     group = 4
     cols = group * SEGP
@@ -143,11 +161,19 @@
     return pl.pallas_call(
         functools.partial(spectra_kernel, chan_count, tm_count),
         out_shape=jax.ShapeDtypeStruct((NFREQ, sub, LANES), jnp.bfloat16),
-        in_specs=[pl.BlockSpec(memory_space=pltpu.SMEM), vmem, vmem, vmem],
+        in_specs=[
+            pl.BlockSpec(memory_space=pltpu.SMEM),
+            vmem,
+            pl.BlockSpec(memory_space=pl.ANY),
+            pl.BlockSpec(memory_space=pl.ANY),
+        ],
         out_specs=vmem,
         scratch_shapes=[
+            pltpu.VMEM(high.shape, high.dtype),
+            pltpu.VMEM(low.shape, low.dtype),
             pltpu.VMEM((NFFT // LANES, sub * SEGP, LANES), jnp.float32),
             pltpu.VMEM((sub * NFREQ, LANES), jnp.float32),
+            pltpu.SemaphoreType.DMA((2,)),
         ],
         compiler_params=pltpu.CompilerParams(vmem_limit_bytes=VMEM_LIMIT),
     )(starts, received, jnp.asarray(high), jnp.asarray(low))
@@ -280,7 +306,25 @@
     )(pairs, owners, jnp.asarray(near), jnp.asarray(reach), jnp.asarray(shell))
 
 
-def exchange_kernel(count, rounds, table_ref, own_ref, out_ref, held, land, stage, send_sem, recv_sem, out_sem):
+def exchange_kernel(
+    count,
+    bands,
+    rounds,
+    table_ref,
+    white_ref,
+    pick_ref,
+    out_ref,
+    held,
+    spread,
+    land,
+    stage,
+    send_sem,
+    recv_sem,
+    out_sem,
+    band_send,
+    band_recv,
+    band_own,
+):
     side = math.isqrt(count)
     me = lax.axis_index("chan")
     x, y = me // side, me % side
@@ -290,15 +334,56 @@
         x * side + (y + side - 1) % side,
         x * side + (y + 1) % side,
     ]
-    rows = own_ref.shape[2]
+    rows = held.shape[2]
+    sub = white_ref.shape[4]
     step = 32
+    band = lax.axis_index("tm")
 
     barrier = pltpu.get_barrier_semaphore()
     for k in range(4):
         pl.semaphore_signal(
             barrier, inc=1, device_id={"chan": targets[k]}, device_id_type=pl.DeviceIdType.MESH
         )
-    pl.semaphore_wait(barrier, 4)
+    for i in range(1, bands):
+        pl.semaphore_signal(
+            barrier, inc=1, device_id={"tm": (band + i) % bands}, device_id_type=pl.DeviceIdType.MESH
+        )
+    pl.semaphore_wait(barrier, 4 + bands - 1)
+
+    def place(source):
+        return pl.ds(pl.multiple_of(source * sub, sub), sub)
+
+    def to_band(h, i):
+        target = (band + i) % bands
+        return pltpu.make_async_remote_copy(
+            src_ref=white_ref.at[target, :, h],
+            dst_ref=spread.at[h, :, :, place(band)],
+            send_sem=band_send.at[h, i],
+            recv_sem=band_recv.at[h, i],
+            device_id={"tm": target},
+            device_id_type=pl.DeviceIdType.MESH,
+        )
+
+    def from_band(h, i):
+        source = (band + bands - i) % bands
+        return pltpu.make_async_remote_copy(
+            src_ref=white_ref.at[source, :, h],
+            dst_ref=spread.at[h, :, :, place(source)],
+            send_sem=band_send.at[h, i],
+            recv_sem=band_recv.at[h, i],
+            device_id={"tm": source},
+            device_id_type=pl.DeviceIdType.MESH,
+        )
+
+    def stay(h):
+        return pltpu.make_async_copy(
+            white_ref.at[band, :, h], spread.at[h, :, :, place(band)], band_own.at[h]
+        )
+
+    for h in range(STREAMS):
+        for i in range(1, bands):
+            to_band(h, i).start()
+        stay(h).start()
 
     def each_chunk(work):
         def run(i, carry):
@@ -319,7 +404,7 @@
 
     def keep_own(h):
         return pltpu.make_async_copy(
-            own_ref.at[:, h], out_ref.at[pl.ds(0, THIRDS), h], out_sem.at[rounds, h]
+            held.at[pl.ds(0, THIRDS), h], out_ref.at[pl.ds(0, THIRDS), h], out_sem.at[rounds, h]
         )
 
     def keep(r, h):
@@ -350,13 +435,23 @@
         for k in range(4):
             remote(parity, h, k).start()
 
+    dims = (((1,), (1,)), ((), ()))
+    quads = spread.shape[2] // QUAD
+
     for h in range(STREAMS):
-
-        def work(at):
-            for s in range(THIRDS):
-                held[s, h, at, :] = own_ref[s, h, at, :]
-
-        each_chunk(work)
+        stay(h).wait()
+        for i in range(1, bands):
+            from_band(h, i).wait_recv()
+
+        def turn(g, carry):
+            s, part = g // quads, g % quads
+            wide = jnp.concatenate([spread[h, s, part * QUAD + q] for q in range(QUAD)], axis=1)
+            value = lax.dot_general(pick_ref[...], wide, dims, preferred_element_type=jnp.float32)
+            at = pl.ds(pl.multiple_of(part * (QUAD * KROWS), QUAD * KROWS), QUAD * KROWS)
+            held[s, h, at, :] = value.astype(jnp.bfloat16)
+            return carry
+
+        lax.fori_loop(0, THIRDS * quads, turn, 0)
         send(0, h)
         keep_own(h).start()
     for h in range(STREAMS):
@@ -378,43 +473,66 @@
             for k in range(4):
                 remote(parity, h, k).wait_send()
     for h in range(STREAMS):
+        for i in range(1, bands):
+            to_band(h, i).wait_send()
         keep_own(h).wait()
         for r in range(rounds):
             keep(r, h).wait()
 
 
-def exchange(table, own, count, rounds, ident):
-    _, streams, rows, block = own.shape
+def exchange(table, white, count, rounds, ident):
+    bands, _, _, freqs, sub, _ = white.shape
+    rows = freqs * KROWS
+    block = bands * sub
+    shape = (THIRDS + 4 * rounds, STREAMS, rows, block)
+    any_space = pl.BlockSpec(memory_space=pl.ANY)
     return pl.pallas_call(
-        functools.partial(exchange_kernel, count, rounds),
-        out_shape=jax.ShapeDtypeStruct((THIRDS * count, streams, rows, block), own.dtype),
-        in_specs=[pl.BlockSpec(memory_space=pltpu.SMEM), pl.BlockSpec(memory_space=pltpu.VMEM)],
-        out_specs=pl.BlockSpec(memory_space=pl.ANY),
+        functools.partial(exchange_kernel, count, bands, rounds),
+        out_shape=jax.ShapeDtypeStruct(shape, white.dtype),
+        in_specs=[
+            pl.BlockSpec(memory_space=pltpu.SMEM),
+            any_space,
+            pl.BlockSpec(memory_space=pltpu.VMEM),
+        ],
+        out_specs=any_space,
         scratch_shapes=[
-            pltpu.VMEM((THIRDS + 4 * rounds, streams, rows, block), own.dtype),
-            pltpu.VMEM((2, streams, 4, rows, block), own.dtype),
-            pltpu.VMEM((2, streams, 4, rows, block), own.dtype),
-            pltpu.SemaphoreType.DMA((2, streams, 4)),
-            pltpu.SemaphoreType.DMA((2, streams, 4)),
-            pltpu.SemaphoreType.DMA((rounds + 1, streams)),
+            pltpu.VMEM(shape, white.dtype),
+            pltpu.VMEM((STREAMS, THIRDS, freqs, block, LANES), white.dtype),
+            pltpu.VMEM((2, STREAMS, 4, rows, block), white.dtype),
+            pltpu.VMEM((2, STREAMS, 4, rows, block), white.dtype),
+            pltpu.SemaphoreType.DMA((2, STREAMS, 4)),
+            pltpu.SemaphoreType.DMA((2, STREAMS, 4)),
+            pltpu.SemaphoreType.DMA((rounds + 1, STREAMS)),
+            pltpu.SemaphoreType.DMA((STREAMS, bands)),
+            pltpu.SemaphoreType.DMA((STREAMS, bands)),
+            pltpu.SemaphoreType.DMA((STREAMS,)),
         ],
         compiler_params=pltpu.CompilerParams(
-            vmem_limit_bytes=VMEM_LIMIT, collective_id=ident, has_side_effects=True
+            vmem_limit_bytes=EXCHANGE_LIMIT, collective_id=ident, has_side_effects=True
         ),
-    )(table, own)
-
-
-def gather_needed(table, slots, rounds, own, me, count):
-    mine = lax.dynamic_index_in_dim(slots, me, 0, keepdims=False)
-    every = np.arange(LANES)
-    every = np.where(every < THIRDS * count, every % count * THIRDS + every // count, 0)
-    every = jnp.asarray(every, jnp.int32)
+    )(table, white, jnp.asarray(pick_table()))
+
+
+def gather_all(white):
+    bands, _, _, freqs, sub, _ = white.shape
+    banded = white.reshape(bands, THIRDS * STREAMS * freqs, sub, LANES)
+    banded = lax.all_to_all(banded, "tm", split_axis=0, concat_axis=0, tiled=True)
+    own = compact(banded).reshape(THIRDS, STREAMS, freqs * KROWS, bands * sub)
+    return lax.all_gather(own, "chan", axis=0, tiled=True)
+
+
+def cross_spectra(table, slot_of, rounds, white, blocks, live, count):
+    thirds = jnp.arange(THIRDS, dtype=jnp.int32)[None, :]
 
     def by_rounds(choice, ident):
-        return lambda: (exchange(table, own, count, choice, ident), mine)
+        def run():
+            held = exchange(table, white, count, choice, ident)
+            return products(held, slot_of[blocks[:, None] + count * thirds], live)
+
+        return run
 
     def whole():
-        return lax.all_gather(own, "chan", axis=0, tiled=True), every
+        return products(gather_all(white), blocks[:, None] * THIRDS + thirds, live)
 
     branches = [by_rounds(choice, i) for i, choice in enumerate(ROUND_CHOICES)] + [whole]
     which = sum((rounds > choice).astype(jnp.int32) for choice in ROUND_CHOICES)
@@ -454,7 +572,7 @@
 
 def products(held, needed, live):
     _, streams, rows, block = held.shape
-    part = streams * rows // KROWS
+    part = streams * (rows // KROWS)
     spec = (1, streams, rows, block)
     return pl.pallas_call(
         product_kernel,
@@ -468,7 +586,7 @@
             ],
             out_specs=pl.BlockSpec((1, part, 2, block, block), lambda s, g, need, live: (s, g, 0, 0, 0)),
         ),
-        compiler_params=pltpu.CompilerParams(vmem_limit_bytes=VMEM_LIMIT),
+        compiler_params=pltpu.CompilerParams(vmem_limit_bytes=PRODUCT_LIMIT),
     )(needed, live, held, held)
 
 
@@ -480,20 +598,17 @@
     sub = block // tm_count
     group_freq = NFREQ // tm_count
     table, slots, rounds = plan(pairs, owners, chan_count)
-    moved = records.reshape(chan_count * tm_count, sub, samp_dev)
+    moved = (records * SCALE).astype(jnp.float16).reshape(chan_count * tm_count, sub, samp_dev)
     received = lax.all_to_all(moved, ("chan", "tm"), split_axis=0, concat_axis=0, tiled=True)
-    white = spectra(starts, received, chan_count, tm_count)
-    white = white.reshape(tm_count, group_freq, sub, LANES)
-    banded = lax.all_to_all(white, "tm", split_axis=0, concat_axis=0, tiled=True)
-    own = compact(banded).reshape(THIRDS, STREAMS, -1, block)
+    white = spectra(starts, received.astype(jnp.float32), chan_count, tm_count)
+    white = white.reshape(tm_count, THIRDS, STREAMS, group_freq // (THIRDS * STREAMS), sub, LANES)
     me_chan = lax.axis_index("chan")
-    held, slot_of = gather_needed(table, slots, rounds[0, 0], own, me_chan, chan_count)
     pair_id, live = slot_table(owners, chan_count)
     mine = lax.dynamic_slice_in_dim(pair_id, me_chan * PMAX, PMAX)
     my_live = lax.dynamic_slice_in_dim(live, me_chan * PMAX, PMAX).astype(jnp.int32)
     blocks = pairs[mine].reshape(2 * PMAX)
-    needed = slot_of[blocks[:, None] + chan_count * jnp.arange(THIRDS, dtype=jnp.int32)[None, :]]
-    return products(held, needed, my_live)
+    slot_of = lax.dynamic_index_in_dim(slots, me_chan, 0, keepdims=False)
+    return cross_spectra(table, slot_of, rounds[0, 0], white, blocks, my_live, chan_count)
 
 
 def solution(mesh):

time: 217 us -> 177 us (0.82)
  blocking collectives: 42.1 us -> 0 us
  Pallas kernels: 140 us -> 132 us
  starting transfers between devices: 4.78 us -> 11.5 us
  other arithmetic: 1.21 us -> 5.04 us
    all_to_all x1 -> x0, blocking collectives: 42.1 us -> none  [body(): lax.all_to_all(moved, ('chan', 'tm'), split_axis=0, concat_axis=0, tiled=...]
    pallas_call x1, Pallas kernels: 26.9 us -> 14.8 us  [products(): pl.pallas_call(product_kernel, out_shape=jax.ShapeDtypeStruct((PMAX, THIR...]
    pallas_call x2 -> x1, Pallas kernels: 81.5 us -> 93.1 us  [exchange(): pl.pallas_call(functools.partial(exchange_kernel, count, bands, rounds),...]
    pallas_call x1, Pallas kernels: 23.7 us -> 16.3 us  [spectra(): pl.pallas_call(functools.partial(spectra_kernel, chan_count, tm_count), o...]
    all_to_all x1, starting transfers between devices: 4.78 us -> 11.5 us  [body(): lax.all_to_all(moved, ('chan', 'tm'), split_axis=0, concat_axis=0, tiled=...]
    convert_element_type x0 -> x2, other arithmetic: none -> 4.42 us  [the longest x1 2.81 us: body(): (records * SCALE).astype(jnp.float16)]
  transfers between devices with their start and end apart: 1 -> 1, of which waited for: 1 -> 1; matrix products, arithmetic and copies ran while one was open for 2% -> 2% of each run, Pallas kernels for 3% -> 4%
where the time goes in v3:
time: 177 us; the launch traced here: 174 us
  Pallas kernels  132 us (75%)
  between operations  14.8 us (8%)
  starting transfers between devices  11.5 us (6%)
  waiting for transfers between devices  7.18 us (4%)
  other arithmetic  5.04 us (3%)
  local copies, waits for them, and re-layouts  3.67 us (2%)
    pallas_call x1, Pallas kernels, exchange(): pl.pallas_call(functools.partial(exchange_kernel, count, bands, rounds),...  93.1 us
    pallas_call x1, Pallas kernels, spectra(): pl.pallas_call(functools.partial(spectra_kernel, chan_count, tm_count), o...  16.3 us
    pallas_call x1, Pallas kernels, products(): pl.pallas_call(product_kernel, out_shape=jax.ShapeDtypeStruct((PMAX, THIR...  14.8 us
    all_to_all x1, starting transfers between devices, body(): lax.all_to_all(moved, ('chan', 'tm'), split_axis=0, concat_axis=0, tiled=...  11.5 us
    pallas_call x1, Pallas kernels, plan(): pl.pallas_call(plan_kernel, out_shape=(grid, grid, jax.ShapeDtypeStruct((...  7.52 us
    all_to_all x1, waiting for transfers between devices, body(): lax.all_to_all(moved, ('chan', 'tm'), split_axis=0, concat_axis=0, tiled=...  7.18 us
  transfers between devices with their start and end apart: 1, of which 1 were waited for; matrix products, arithmetic and copies ran while one was open for 2% of the time, Pallas kernels for 4%

profile of v3, /device:TPU:1, one launch (start us, length us, event | category | flops | bytes accessed | tf_op | source)
XLA Modules:
  0.0 173.9 jit_solution(5637094712235747366)
XLA Ops:
  6.5 0.0 copy-start.3
  6.5 0.0 copy-start.4
  6.5 2.8 %multiply_convert_fusion = f16[2048,256]{1,0:T(8,128)(2,1)} fusion(f32[2048,256]{1,0:T(8,128)} %param.15), kind=kLoop, calls=%fused_computation.13 | loop fusion | flops 1048576 | bytes 3145728 | tf_op jit(solution)/shard_map/convert_element_type | solution.py:601
  9.3 11.5 %all-to-all-start.1 = ((f16[128,16,256]{2,1,0:T(8,128)(2,1)}), f16[128,16,256]{2,1,0:T(8,128)(2,1)S(1)}, u32[]{:S(2)}, u32[]{:S(2)}) async-start(f16[128,16,256]{2,1,0:T(8,128)(2,1)} %bitcast.11), calls=%async_computation.1 | async-start | bytes 2097152 | tf_op jit(solution)/shard_map/all_to_all | solution.py:602
  20.9 0.0 copy-done.3
  20.9 0.1 copy.25.pairs_ref
  21.0 0.0 copy-done.4
  21.0 0.0 copy-start.2
  21.0 0.7 copy.26.owners_ref
  21.7 0.2 convert_reduce_fusion
  21.8 0.1 select_reduce_fusion
  21.9 0.1 compare_select_fusion.2
  22.0 0.6 gather_fusion.2
  22.6 0.0 copy-done.2
  22.6 7.5 %shard_map.121 = (s32[16,128]{1,0:T(8,128)S(1)}, s32[16,128]{1,0:T(8,128)S(1)}, s32[8,128]{1,0:T(8,128)}) custom-call(s32[48,2]{1,0:T(8,128)} %copy-done.2, s32[48,1]{1,0:T(8,128)} %copy.26.owners_ref, bf16[64,16]{1,0:T(8,128)(2,1)} %constant.60.clone.near_ref, bf16[64,16]{1,0:T(8,128)(2,1)} %constant.61.clone.reach_ref, bf16[16,64]{1,0:T(8,128)(2,1)} %constant.62.clone.shell_ref), custom_call_target="tpu_custom_call" | custom-call | tf_op jit(solution)/shard_map/pallas_call | solution.py:301
  30.1 1.3 slice.3
  32.8 0.1 fusion
  32.9 0.1 dynamic-slice_convert_fusion
  33.0 7.2 %all-to-all-done.1 = f16[128,16,256]{2,1,0:T(8,128)(2,1)S(1)} async-done(((f16[128,16,256]{2,1,0:T(8,128)(2,1)}), f16[128,16,256]{2,1,0:T(8,128)(2,1)S(1)}, u32[]{:S(2)}, u32[]{:S(2)}) %all-to-all-start.1) | async-done | bytes 1048608 | tf_op jit(solution)/shard_map/all_to_all | solution.py:602
  40.1 1.6 convert_element_type.24.rec_ref
  41.7 0.0 copy-start.1
  41.7 16.3 %shard_map.122 = bf16[384,16,128]{2,1,0:T(8,128)(2,1)S(1)} custom-call(s32[58]{0:T(128)} %starts_ref.1, f32[128,16,256]{2,1,0:T(8,128)} %convert_element_type.24.rec_ref, bf16[768,1024]{1,0:T(8,128)(2,1)} %constant.63.clone.high_hbm, bf16[768,1024]{1,0:T(8,128)(2,1)} %constant.64.clone.low_hbm), custom_call_target="tpu_custom_call" | custom-call | tf_op jit(solution)/shard_map/pallas_call | solution.py:161
  58.0 0.0 copy-done.1
  58.0 109.0 %conditional.1 = (bf16[6,48,2,128,128]{4,3,2,1,0:T(8,128)(2,1)}) conditional(s32[]{:T(128)} %bitcast.9, (s32[6,2]{1,0:T(8,128)S(1)}, s32[1,3]{1,0:T(1,128)S(1)}, s32[16,128]{1,0:T(8,128)S(1)}, s32[16,128]{1,0:T(8,128)S(1)}, bf16[384,16,128]{2,1,0:T(8,128)(2,1)S(1)}, /*index=5*/bf16[464,512]{1,0:T(8,128)(2,1)S(1)}, s32[6]{0:T(128)S(1)}, ...), branch_computations={%region_3.4_spmd, %region_4.5_spmd, %region_5.6_spmd} | conditional | flops 1174 | bytes 167068096 | solution.py:539
  58.1 0.1 add.84
  58.2 0.1 compare_select_fusion
  58.2 0.1 reshape.173
  58.3 0.8 gather_fusion
  59.1 0.1 reshape.172.needed_ref
  59.2 93.1 %branch_0_fun.2.left_ref.right_ref = bf16[31,2,928,128]{3,2,1,0:T(8,128)(2,1)S(1)} custom-call(s32[16,128]{1,0:T(8,128)S(1)} %get-tuple-element.51.table_ref, bf16[8,3,2,8,16,128]{5,4,3,2,1,0:T(8,128)(2,1)S(1)} %bitcast.21, bf16[464,512]{1,0:T(8,128)(2,1)S(1)} %get-tuple-element.53.pick_ref), custom_call_target="tpu_custom_call" | custom-call | tf_op jit(solution)/shard_map/cond/branch_0_fun/pallas_call | solution.py:489
  152.3 14.8 %branch_0_fun.3 = bf16[6,48,2,128,128]{4,3,2,1,0:T(8,128)(2,1)} custom-call(s32[12,3]{1,0:T(8,128)S(1)} %reshape.172.needed_ref, s32[6]{0:T(128)S(1)} %get-tuple-element.50.live_ref, bf16[31,2,928,128]{3,2,1,0:T(8,128)(2,1)S(1)} %branch_0_fun.2.left_ref.right_ref, bf16[31,2,928,128]{3,2,1,0:T(8,128)(2,1)S(1)} %branch_0_fun.2.left_ref.right_ref), custom_call_target="tpu_custom_call" | custom-call | tf_op jit(solution)/shard_map/cond/branch_0_fun/pallas_call | solution.py:577
  (7 shorter events, 0.0 us)
Async XLA Ops:
  6.5 14.3 %copy-start.3 = (s32[48,2]{0,1:T(2,128)S(1)}, s32[48,2]{0,1:T(2,128)}, u32[]{:S(2)}) copy-start(s32[48,2]{0,1:T(2,128)} %param.16) | copy-start | bytes 1156
  6.5 14.4 %copy-start.4 = (s32[48,1]{0,1:T(1,128)S(1)}, s32[48,1]{0,1:T(1,128)}, u32[]{:S(2)}) copy-start(s32[48,1]{0,1:T(1,128)} %param.17) | copy-start | bytes 580
  9.3 30.8 %all-to-all-start.1 = ((f16[128,16,256]{2,1,0:T(8,128)(2,1)}), f16[128,16,256]{2,1,0:T(8,128)(2,1)S(1)}, u32[]{:S(2)}, u32[]{:S(2)}) async-start(f16[128,16,256]{2,1,0:T(8,128)(2,1)} %bitcast.11), calls=%async_computation.1 | async-start | bytes 2097152 | tf_op jit(solution)/shard_map/all_to_all | solution.py:602
  21.0 1.6 copy-start.2
  41.7 16.3 %copy-start.1 = (bf16[464,512]{1,0:T(8,128)(2,1)S(1)}, bf16[464,512]{1,0:T(8,128)(2,1)}, u32[]{:S(2)}) copy-start(bf16[464,512]{1,0:T(8,128)(2,1)} %constant.65.clone) | copy-start | bytes 1425412

commit v4 on v3

--- a/solution.py
+++ b/solution.py
@@ -24,7 +24,8 @@
 THIRDS = 3
 STREAMS = 2
 MAX_ROUNDS = 32
-ROUND_CHOICES = (7, 8)
+ROUND_CHOICES = (7, 8, 9)
+RULES = (3, 7)
 SCALE = 8192.0
 
 
@@ -104,7 +105,9 @@
             frames[j, pl.ds(s, sub, stride=SEGP), :] = jnp.where(keep, turned[j], turned[j + 1])
         return carry
 
-    lax.fori_loop(0, SEG, cut, 0, unroll=2)
+    lax.fori_loop(0, SEG // 4 * 4, cut, 0, unroll=4)
+    for s in range(SEG // 4 * 4, SEG):
+        cut(s, 0)
     for copy in fetch:
         copy.wait()
 
@@ -143,7 +146,7 @@
             spread[pl.ds(odd, NFREQ), :] = jnp.where(half, pltpu.roll(a, SEGP, 1), b)
         return carry
 
-    lax.fori_loop(0, sub // group, transform, 0)
+    lax.fori_loop(0, sub // group, transform, 0, unroll=2)
 
     def regroup(f, carry):
         for u in range(8):
@@ -151,7 +154,7 @@
             out_ref[k] = spread[pl.ds(k, sub, stride=NFREQ), :].astype(jnp.bfloat16)
         return carry
 
-    lax.fori_loop(0, NFREQ // 8, regroup, 0)
+    lax.fori_loop(0, NFREQ // 8, regroup, 0, unroll=4)
 
 
 def spectra(starts, received, chan_count, tm_count):
@@ -221,25 +224,29 @@
         x * side + (y + 1) % side,
         x * side + (y - 1) % side,
     ]
-    near = np.concatenate([np.eye(count)[source] for source in sources], axis=0)
+    every = np.eye(len(RULES))
+    near = np.concatenate([np.kron(every, np.eye(count)[source]) for source in sources], axis=0)
     dx = np.abs(x[:, None] - x[None, :])
     dy = np.abs(y[:, None] - y[None, :])
     dist = np.minimum(dx, side - dx) + np.minimum(dy, side - dy)
-    reach = np.concatenate([dist <= d for d in range(4)], axis=0)
-    shell = np.concatenate([(dist == d) * 2.0 ** (3 - d) for d in range(4)], axis=1)
+    reach = np.concatenate([np.kron(every, dist <= d) for d in range(4)], axis=0)
+    shell = np.concatenate([np.kron(every, (dist == d) * 2.0 ** (3 - d)) for d in range(4)], axis=1)
     return [t.astype(ml_dtypes.bfloat16) for t in (near, reach, shell)]
 
 
 def plan_kernel(pairs_ref, owners_ref, near_ref, reach_ref, shell_ref, table_ref, slots_ref, rounds_ref):
-    count = near_ref.shape[1]
-    shape = (count, LANES)
-    node = lax.broadcasted_iota(jnp.int32, shape, 0)
+    rows = near_ref.shape[1]
+    count = rows // len(RULES)
+    shape = (rows, LANES)
+    row = lax.broadcasted_iota(jnp.int32, shape, 0)
+    node = row % count
+    turn = jnp.where(row < count, RULES[0], RULES[1])
     lane = lax.broadcasted_iota(jnp.int32, shape, 1)
     inside = lane < THIRDS * count
     block = lane % count
     third = lane // count
     commodities = THIRDS * count
-    tie = commodities - 1 - (lane + 3 * node) % commodities
+    tie = commodities - 1 - (lane + turn * node) % commodities
     tie = jnp.where(inside, tie, 0).astype(jnp.float32)
 
     def mark(p, need):
@@ -264,14 +271,15 @@
         short = rem * jnp.sum(rem, axis=1, keepdims=True)
         reached = dot(reach_ref[...], has)
         waves = jnp.concatenate(
-            [jnp.where(reached[d * count : (d + 1) * count] > 0, 0.0, short) for d in range(4)], axis=0
+            [jnp.where(reached[d * rows : (d + 1) * rows] > 0, 0.0, short) for d in range(4)], axis=0
         )
         gain = dot(shell_ref[...], waves)
         both = dot(near_ref[...], jnp.concatenate([has, slot_of], axis=1))
-        near_has = [both[k * count : (k + 1) * count, :LANES] for k in range(4)]
-        near_slot = [both[k * count : (k + 1) * count, LANES:] for k in range(4)]
+        near_has = [both[k * rows : (k + 1) * rows, :LANES] for k in range(4)]
+        near_slot = [both[k * rows : (k + 1) * rows, LANES:] for k in range(4)]
         sources = near_has[0] + near_has[1] + near_has[2] + near_has[3]
-        worth = jnp.where((gain > 0) & (has == 0), gain * (5.0 - sources) * 64.0 + tie, 0.0)
+        scarce = 5.0 - sources
+        worth = jnp.where((gain > 0) & (has == 0), gain * scarce * scarce * 64.0 + tie, 0.0)
         for k in range(4):
             key = worth * near_has[k]
             best = jnp.max(key, axis=1, keepdims=True)
@@ -281,15 +289,18 @@
             source = jnp.sum(jnp.where(chosen, near_slot[k], 0.0), axis=1, keepdims=True)
             table = jnp.where(lane == 4 * r + k, source, table)
             slot_of = jnp.where(chosen, (THIRDS + 4 * r + k).astype(jnp.float32), slot_of)
-        left = jnp.sum(need * (1.0 - has))
-        return r + 1, left, has, slot_of, table
-
-    left = jnp.sum(need * (1.0 - has))
+        return r + 1, jnp.minimum(*missing(has)), has, slot_of, table
+
+    def missing(has):
+        rem = need * (1.0 - has)
+        return jnp.sum(rem[:count]), jnp.sum(rem[count:])
+
     rounds, left, has, slot_of, table = lax.while_loop(
-        unfinished, one, (jnp.int32(0), left, has, slot_of, table)
+        unfinished, one, (jnp.int32(0), jnp.float32(1.0), has, slot_of, table)
     )
-    table_ref[...] = table.astype(jnp.int32)
-    slots_ref[...] = slot_of.astype(jnp.int32)
+    first = missing(has)[0] == 0
+    table_ref[...] = jnp.where(first, table[:count], table[count:]).astype(jnp.int32)
+    slots_ref[...] = jnp.where(first, slot_of[:count], slot_of[count:]).astype(jnp.int32)
     rounds_ref[...] = jnp.full(rounds_ref.shape, jnp.where(left > 0, MAX_ROUNDS, rounds), jnp.int32)
 
 
@@ -563,7 +574,7 @@
                 out_ref[0, g * QUAD + q, 1] = value[:, block:]
             return carry
 
-        lax.fori_loop(0, streams * per, one, 0)
+        lax.fori_loop(0, streams * per, one, 0, unroll=True)
 
     @pl.when(live_ref[slot] == 0)
     def _():

time: 177 us -> 181 us (1.023); the launches traced: 174 us -> 180 us
  Pallas kernels: 132 us -> 139 us
    pallas_call x1, Pallas kernels: 93.1 us -> 103 us  [exchange(): pl.pallas_call(functools.partial(exchange_kernel, count, bands, rounds),...]
    pallas_call x1, Pallas kernels: 14.8 us -> 12.7 us  [products(): pl.pallas_call(product_kernel, out_shape=jax.ShapeDtypeStruct((PMAX, THIR...]
    pallas_call x1, Pallas kernels: 16.3 us -> 14.4 us  [spectra(): pl.pallas_call(functools.partial(spectra_kernel, chan_count, tm_count), o...]
  transfers between devices with their start and end apart: 1 -> 1, of which waited for: 1 -> 1; matrix products, arithmetic and copies ran while one was open for 2% -> 2% of each run, Pallas kernels for 4% -> 5%
where the time goes in v4:
time: 181 us; the launch traced here: 180 us
  Pallas kernels  139 us (77%)
  between operations  15.1 us (8%)
  starting transfers between devices  11.5 us (6%)
  waiting for transfers between devices  6.18 us (3%)
  other arithmetic  5.04 us (3%)
  local copies, waits for them, and re-layouts  3.57 us (2%)
    pallas_call x1, Pallas kernels, exchange(): pl.pallas_call(functools.partial(exchange_kernel, count, bands, rounds),...  103 us
    pallas_call x1, Pallas kernels, spectra(): pl.pallas_call(functools.partial(spectra_kernel, chan_count, tm_count), o...  14.4 us
    pallas_call x1, Pallas kernels, products(): pl.pallas_call(product_kernel, out_shape=jax.ShapeDtypeStruct((PMAX, THIR...  12.7 us
    all_to_all x1, starting transfers between devices, body(): lax.all_to_all(moved, ('chan', 'tm'), split_axis=0, concat_axis=0, tiled=...  11.5 us
    pallas_call x1, Pallas kernels, plan(): pl.pallas_call(plan_kernel, out_shape=(grid, grid, jax.ShapeDtypeStruct((...  8.31 us
    all_to_all x1, waiting for transfers between devices, body(): lax.all_to_all(moved, ('chan', 'tm'), split_axis=0, concat_axis=0, tiled=...  6.18 us
  transfers between devices with their start and end apart: 1, of which 1 were waited for; matrix products, arithmetic and copies ran while one was open for 2% of the time, Pallas kernels for 5%

profile of v4, /device:TPU:1, one launch (start us, length us, event | category | flops | bytes accessed | tf_op | source)
XLA Modules:
  0.0 180.1 jit_solution(2916607632537480085)
XLA Ops:
  6.5 0.0 copy-start.3
  6.5 0.0 copy-start.4
  6.5 2.8 %multiply_convert_fusion = f16[2048,256]{1,0:T(8,128)(2,1)} fusion(f32[2048,256]{1,0:T(8,128)} %param.17), kind=kLoop, calls=%fused_computation.18 | loop fusion | flops 1048576 | bytes 3145728 | tf_op jit(solution)/shard_map/convert_element_type | solution.py:612
  9.3 11.5 %all-to-all-start.1 = ((f16[128,16,256]{2,1,0:T(8,128)(2,1)}), f16[128,16,256]{2,1,0:T(8,128)(2,1)S(1)}, u32[]{:S(2)}, u32[]{:S(2)}) async-start(f16[128,16,256]{2,1,0:T(8,128)(2,1)} %bitcast.14), calls=%async_computation.1 | async-start | bytes 2097152 | tf_op jit(solution)/shard_map/all_to_all | solution.py:613
  20.9 0.0 copy-done.3
  20.9 0.1 copy.27.pairs_ref
  21.0 0.0 copy-done.4
  21.0 0.0 copy-start.2
  21.0 0.7 copy.28.owners_ref
  21.7 0.2 convert_reduce_fusion
  21.8 0.1 select_reduce_fusion
  21.9 0.1 compare_select_fusion.3
  22.0 0.6 gather_fusion.3
  22.6 0.0 copy-done.2
  22.6 8.3 %shard_map.131 = (s32[16,128]{1,0:T(8,128)S(1)}, s32[16,128]{1,0:T(8,128)S(1)}, s32[8,128]{1,0:T(8,128)}) custom-call(s32[48,2]{1,0:T(8,128)} %copy-done.2, s32[48,1]{1,0:T(8,128)} %copy.28.owners_ref, bf16[128,32]{1,0:T(8,128)(2,1)} %constant.66.clone.near_ref, bf16[128,32]{1,0:T(8,128)(2,1)} %constant.67.clone.reach_ref, ...), custom_call_target="tpu_custom_call" | custom-call | tf_op jit(solution)/shard_map/pallas_call | solution.py:312
  30.9 1.2 slice.3
  33.8 0.1 fusion
  33.9 0.1 dynamic-slice_convert_fusion
  33.9 6.2 %all-to-all-done.1 = f16[128,16,256]{2,1,0:T(8,128)(2,1)S(1)} async-done(((f16[128,16,256]{2,1,0:T(8,128)(2,1)}), f16[128,16,256]{2,1,0:T(8,128)(2,1)S(1)}, u32[]{:S(2)}, u32[]{:S(2)}) %all-to-all-start.1) | async-done | bytes 1048608 | tf_op jit(solution)/shard_map/all_to_all | solution.py:613
  40.1 1.6 convert_element_type.29.rec_ref
  41.7 0.0 copy-start.1
  41.7 14.4 %shard_map.132 = bf16[384,16,128]{2,1,0:T(8,128)(2,1)S(1)} custom-call(s32[58]{0:T(128)} %starts_ref.1, f32[128,16,256]{2,1,0:T(8,128)} %convert_element_type.29.rec_ref, bf16[768,1024]{1,0:T(8,128)(2,1)} %constant.69.clone.high_hbm, bf16[768,1024]{1,0:T(8,128)(2,1)} %constant.70.clone.low_hbm), custom_call_target="tpu_custom_call" | custom-call | tf_op jit(solution)/shard_map/pallas_call | solution.py:164
  56.2 0.0 copy-done.1
  56.2 117.1 %conditional.1 = (bf16[6,48,2,128,128]{4,3,2,1,0:T(8,128)(2,1)}) conditional(s32[]{:T(128)} %bitcast.12, (s32[6,2]{1,0:T(8,128)S(1)}, s32[1,3]{1,0:T(1,128)S(1)}, s32[16,128]{1,0:T(8,128)S(1)}, s32[16,128]{1,0:T(8,128)S(1)}, bf16[384,16,128]{2,1,0:T(8,128)(2,1)S(1)}, /*index=5*/bf16[464,512]{1,0:T(8,128)(2,1)S(1)}, ...), branch_computations={%region_3.4_spmd, %region_4.5_spmd, %region_5.6_spmd, %region_6.7_... | conditional | flops 1174 | bytes 167068096 | solution.py:550
  56.2 0.1 add.122
  56.3 0.1 compare_select_fusion.1
  56.4 0.1 reshape.251
  56.5 0.8 gather_fusion.1
  57.3 0.1 reshape.250.needed_ref
  57.4 103.3 %branch_1_fun.2.left_ref.right_ref = bf16[35,2,928,128]{3,2,1,0:T(8,128)(2,1)S(1)} custom-call(s32[16,128]{1,0:T(8,128)S(1)} %get-tuple-element.73.table_ref, bf16[8,3,2,8,16,128]{5,4,3,2,1,0:T(8,128)(2,1)S(1)} %bitcast.29, bf16[464,512]{1,0:T(8,128)(2,1)S(1)} %get-tuple-element.75.pick_ref), custom_call_target="tpu_custom_call" | custom-call | tf_op jit(solution)/shard_map/cond/branch_1_fun/pallas_call | solution.py:500
  160.6 12.7 %branch_1_fun.3 = bf16[6,48,2,128,128]{4,3,2,1,0:T(8,128)(2,1)} custom-call(s32[12,3]{1,0:T(8,128)S(1)} %reshape.250.needed_ref, s32[6]{0:T(128)S(1)} %get-tuple-element.72.live_ref, bf16[35,2,928,128]{3,2,1,0:T(8,128)(2,1)S(1)} %branch_1_fun.2.left_ref.right_ref, bf16[35,2,928,128]{3,2,1,0:T(8,128)(2,1)S(1)} %branch_1_fun.2.left_ref.right_ref), custom_call_target="tpu_custom_call" | custom-call | tf_op jit(solution)/shard_map/cond/branch_1_fun/pallas_call | solution.py:588
  (7 shorter events, 0.0 us)
Async XLA Ops:
  6.5 14.3 %copy-start.3 = (s32[48,2]{0,1:T(2,128)S(1)}, s32[48,2]{0,1:T(2,128)}, u32[]{:S(2)}) copy-start(s32[48,2]{0,1:T(2,128)} %param.18) | copy-start | bytes 1156
  6.5 14.4 %copy-start.4 = (s32[48,1]{0,1:T(1,128)S(1)}, s32[48,1]{0,1:T(1,128)}, u32[]{:S(2)}) copy-start(s32[48,1]{0,1:T(1,128)} %param.19) | copy-start | bytes 580
  9.3 30.8 %all-to-all-start.1 = ((f16[128,16,256]{2,1,0:T(8,128)(2,1)}), f16[128,16,256]{2,1,0:T(8,128)(2,1)S(1)}, u32[]{:S(2)}, u32[]{:S(2)}) async-start(f16[128,16,256]{2,1,0:T(8,128)(2,1)} %bitcast.14), calls=%async_computation.1 | async-start | bytes 2097152 | tf_op jit(solution)/shard_map/all_to_all | solution.py:613
  21.0 1.6 copy-start.2
  41.7 14.4 %copy-start.1 = (bf16[464,512]{1,0:T(8,128)(2,1)S(1)}, bf16[464,512]{1,0:T(8,128)(2,1)}, u32[]{:S(2)}) copy-start(bf16[464,512]{1,0:T(8,128)(2,1)} %constant.71.clone) | copy-start | bytes 1425412

commit v5 on v4

--- a/solution.py
+++ b/solution.py
@@ -22,7 +22,9 @@
 EXCHANGE_LIMIT = 28 * 1024 * 1024
 PRODUCT_LIMIT = 12 * 1024 * 1024
 THIRDS = 3
-STREAMS = 2
+STREAMS = 4
+DELAYS = (0, 0, 1, 1)
+LEAD = 2
 MAX_ROUNDS = 32
 ROUND_CHOICES = (7, 8, 9)
 RULES = (3, 7)
@@ -347,7 +349,7 @@
     ]
     rows = held.shape[2]
     sub = white_ref.shape[4]
-    step = 32
+    step = 16
     band = lax.axis_index("tm")
 
     barrier = pltpu.get_barrier_semaphore()
@@ -364,34 +366,30 @@
     def place(source):
         return pl.ds(pl.multiple_of(source * sub, sub), sub)
 
-    def to_band(h, i):
-        target = (band + i) % bands
+    def band_copy(h, i, source, target, peer):
         return pltpu.make_async_remote_copy(
             src_ref=white_ref.at[target, :, h],
-            dst_ref=spread.at[h, :, :, place(band)],
-            send_sem=band_send.at[h, i],
-            recv_sem=band_recv.at[h, i],
-            device_id={"tm": target},
-            device_id_type=pl.DeviceIdType.MESH,
-        )
-
-    def from_band(h, i):
-        source = (band + bands - i) % bands
-        return pltpu.make_async_remote_copy(
-            src_ref=white_ref.at[source, :, h],
             dst_ref=spread.at[h, :, :, place(source)],
             send_sem=band_send.at[h, i],
             recv_sem=band_recv.at[h, i],
-            device_id={"tm": source},
+            device_id={"tm": peer},
             device_id_type=pl.DeviceIdType.MESH,
         )
+
+    def to_band(h, i):
+        target = (band + i) % bands
+        return band_copy(h, i, band, target, target)
+
+    def from_band(h, i):
+        source = (band + bands - i) % bands
+        return band_copy(h, i, source, source, source)
 
     def stay(h):
         return pltpu.make_async_copy(
             white_ref.at[band, :, h], spread.at[h, :, :, place(band)], band_own.at[h]
         )
 
-    for h in range(STREAMS):
+    def spread_out(h):
         for i in range(1, bands):
             to_band(h, i).start()
         stay(h).start()
@@ -449,10 +447,12 @@
     dims = (((1,), (1,)), ((), ()))
     quads = spread.shape[2] // QUAD
 
-    for h in range(STREAMS):
+    def begin(h):
         stay(h).wait()
         for i in range(1, bands):
             from_band(h, i).wait_recv()
+        if h + LEAD < STREAMS:
+            spread_out(h + LEAD)
 
         def turn(g, carry):
             s, part = g // quads, g % quads
@@ -465,25 +465,47 @@
         lax.fori_loop(0, THIRDS * quads, turn, 0)
         send(0, h)
         keep_own(h).start()
-    for h in range(STREAMS):
+
+    def free(parity, h):
+        for k in range(4):
+            remote(parity, h, k).wait_send()
+
+    def advance(r, h):
+        absorb(r - 1, h)
+        free(r % 2, h)
+        send(r, h)
+
+    def second(h):
         absorb(0, h)
         send(1, h)
 
-    def general(r, carry):
+    for h in range(LEAD):
+        spread_out(h)
+    peeled = max(DELAYS) + 2
+    for t in range(peeled):
         for h in range(STREAMS):
-            absorb(r - 1, h)
-            for k in range(4):
-                remote(r % 2, h, k).wait_send()
-            send(r, h)
+            if t - DELAYS[h] == 0:
+                begin(h)
+            elif t - DELAYS[h] == 1:
+                second(h)
+            elif t - DELAYS[h] > 1:
+                advance(t - DELAYS[h], h)
+
+    def general(t, carry):
+        for h in range(STREAMS):
+            advance(t - DELAYS[h], h)
         return carry
 
-    lax.fori_loop(2, rounds, general, 0)
+    lax.fori_loop(peeled, rounds, general, 0)
+    for t in range(rounds, rounds + max(DELAYS) + 1):
+        for h in range(STREAMS):
+            if t - DELAYS[h] == rounds:
+                absorb(rounds - 1, h)
+            elif t - DELAYS[h] < rounds:
+                advance(t - DELAYS[h], h)
     for h in range(STREAMS):
-        absorb(rounds - 1, h)
         for parity in range(2):
-            for k in range(4):
-                remote(parity, h, k).wait_send()
-    for h in range(STREAMS):
+            free(parity, h)
         for i in range(1, bands):
             to_band(h, i).wait_send()
         keep_own(h).wait()
@@ -529,21 +551,27 @@
     banded = white.reshape(bands, THIRDS * STREAMS * freqs, sub, LANES)
     banded = lax.all_to_all(banded, "tm", split_axis=0, concat_axis=0, tiled=True)
     own = compact(banded).reshape(THIRDS, STREAMS, freqs * KROWS, bands * sub)
-    return lax.all_gather(own, "chan", axis=0, tiled=True)
+    count = lax.axis_size("chan")
+    copies = jnp.broadcast_to(own[None], (count,) + own.shape)
+    copies = lax.all_to_all(copies, "chan", split_axis=0, concat_axis=0, tiled=True)
+    return copies.reshape((count * THIRDS,) + own.shape[1:])
 
 
 def cross_spectra(table, slot_of, rounds, white, blocks, live, count):
     thirds = jnp.arange(THIRDS, dtype=jnp.int32)[None, :]
+    chosen = slot_of[blocks[:, None] + count * thirds]
+    everywhere = blocks[:, None] * THIRDS + thirds
+    chosen, everywhere, live, white = lax.optimization_barrier((chosen, everywhere, live, white))
 
     def by_rounds(choice, ident):
         def run():
             held = exchange(table, white, count, choice, ident)
-            return products(held, slot_of[blocks[:, None] + count * thirds], live)
+            return products(held, chosen, live)
 
         return run
 
     def whole():
-        return products(gather_all(white), blocks[:, None] * THIRDS + thirds, live)
+        return products(gather_all(white), everywhere, live)
 
     branches = [by_rounds(choice, i) for i, choice in enumerate(ROUND_CHOICES)] + [whole]
     which = sum((rounds > choice).astype(jnp.int32) for choice in ROUND_CHOICES)

time: 181 us -> 154 us (0.85)
  between operations: 15.1 us -> 1.98 us
  Pallas kernels: 139 us -> 127 us
  waiting for transfers between devices: 6.18 us -> 1.9 us
  local copies, waits for them, and re-layouts: 3.57 us -> 5.6 us
    pallas_call x1, Pallas kernels: 103 us -> 90.7 us  [exchange(): pl.pallas_call(functools.partial(exchange_kernel, count, bands, rounds),...]
    all_to_all x1, waiting for transfers between devices: 6.18 us -> 1.9 us  [body(): lax.all_to_all(moved, ('chan', 'tm'), split_axis=0, concat_axis=0, tiled=...]
  transfers between devices with their start and end apart: 1 -> 1, of which waited for: 1 -> 1; matrix products, arithmetic and copies ran while one was open for 2% -> 5% of each run, Pallas kernels for 5% -> 5%
where the time goes in v5:
time: 154 us; the launch traced here: 155 us
  Pallas kernels  127 us (82%)
  starting transfers between devices  11.5 us (7%)
  other arithmetic  6.54 us (4%)
  local copies, waits for them, and re-layouts  5.6 us (4%)
  between operations  1.98 us (1%)
  waiting for transfers between devices  1.9 us (1%)
    pallas_call x1, Pallas kernels, exchange(): pl.pallas_call(functools.partial(exchange_kernel, count, bands, rounds),...  90.7 us
    pallas_call x1, Pallas kernels, spectra(): pl.pallas_call(functools.partial(spectra_kernel, chan_count, tm_count), o...  14.3 us
    pallas_call x1, Pallas kernels, products(): pl.pallas_call(product_kernel, out_shape=jax.ShapeDtypeStruct((PMAX, THIR...  14.2 us
    all_to_all x1, starting transfers between devices, body(): lax.all_to_all(moved, ('chan', 'tm'), split_axis=0, concat_axis=0, tiled=...  11.5 us
    pallas_call x1, Pallas kernels, plan(): pl.pallas_call(plan_kernel, out_shape=(grid, grid, jax.ShapeDtypeStruct((...  7.73 us
  transfers between devices with their start and end apart: 1, of which 1 were waited for; matrix products, arithmetic and copies ran while one was open for 5% of the time, Pallas kernels for 5%

profile of v5, /device:TPU:1, one launch (start us, length us, event | category | flops | bytes accessed | tf_op | source)
XLA Modules:
  0.0 154.5 jit_solution(7829465397384371022)
XLA Ops:
  0.0 0.0 copy-start
  0.0 2.8 %multiply_convert_fusion = f16[2048,256]{1,0:T(8,128)(2,1)} fusion(f32[2048,256]{1,0:T(8,128)} %param.17), kind=kLoop, calls=%fused_computation.2 | loop fusion | flops 1048576 | bytes 3145728 | tf_op jit(solution)/shard_map/convert_element_type | solution.py:640
  2.8 11.5 %all-to-all-start.2 = ((f16[128,16,256]{2,1,0:T(8,128)(2,1)}), f16[128,16,256]{2,1,0:T(8,128)(2,1)S(1)}, u32[]{:S(2)}, u32[]{:S(2)}) async-start(f16[128,16,256]{2,1,0:T(8,128)(2,1)} %bitcast.6), calls=%async_computation.2 | async-start | bytes 2097152 | tf_op jit(solution)/shard_map/all_to_all | solution.py:641
  14.4 1.3 copy.25.owners_ref
  15.7 0.9 convert_reduce_fusion
  16.6 0.7 multiply_add_fusion
  17.3 0.1 select_reduce_fusion
  17.4 0.1 compare_select_fusion.1
  17.5 0.8 copy.24.pairs_ref
  18.2 0.0 copy-start.1
  18.2 0.6 gather_fusion
  18.8 0.1 add.83
  18.9 0.1 compare_select_fusion
  18.9 0.1 reshape.117
  19.0 0.0 copy-done.1
  19.0 7.7 %shard_map.131 = (s32[16,128]{1,0:T(8,128)S(1)}, s32[16,128]{1,0:T(8,128)}, s32[8,128]{1,0:T(8,128)}) custom-call(s32[48,2]{1,0:T(8,128)} %copy-done.1, s32[48,1]{1,0:T(8,128)} %copy.25.owners_ref, bf16[128,32]{1,0:T(8,128)(2,1)} %constant.18.clone.near_ref, bf16[128,32]{1,0:T(8,128)(2,1)} %constant.52.clone.reach_ref, bf16[32,128]{1,0:T(8,128)(2,1)} %constant.53.clone.shell_ref), custom_call_target="tpu_custom_call" | custom-call | tf_op jit(solution)/shard_map/pallas_call | solution.py:314
  26.8 1.2 slice.3
  29.9 0.7 dynamic-slice_bitcast_fusion
  30.6 0.8 gather_fusion.1
  31.4 0.1 reshape.116
  31.5 0.1 fusion
  31.6 0.1 dynamic-slice_convert_fusion
  31.6 0.1 iota_add_fusion
  31.7 1.9 %all-to-all-done.2 = f16[128,16,256]{2,1,0:T(8,128)(2,1)S(1)} async-done(((f16[128,16,256]{2,1,0:T(8,128)(2,1)}), f16[128,16,256]{2,1,0:T(8,128)(2,1)S(1)}, u32[]{:S(2)}, u32[]{:S(2)}) %all-to-all-start.2) | async-done | bytes 1048608 | tf_op jit(solution)/shard_map/all_to_all | solution.py:641
  33.6 1.6 %convert_element_type.30.rec_ref = f32[128,16,256]{2,1,0:T(8,128)} convert(f16[128,16,256]{2,1,0:T(8,128)(2,1)S(1)} %all-to-all-done.2) | non-fusion elementwise | flops 524288 | bytes 3145728 | tf_op jit(solution)/shard_map/convert_element_type | solution.py:642
  35.2 14.3 %shard_map.132 = bf16[384,16,128]{2,1,0:T(8,128)(2,1)S(1)} custom-call(s32[58]{0:T(128)} %starts_ref.1, f32[128,16,256]{2,1,0:T(8,128)} %convert_element_type.30.rec_ref, bf16[768,1024]{1,0:T(8,128)(2,1)} %constant.54.clone.high_hbm, bf16[768,1024]{1,0:T(8,128)(2,1)} %constant.55.clone.low_hbm), custom_call_target="tpu_custom_call" | custom-call | tf_op jit(solution)/shard_map/pallas_call | solution.py:166
  49.6 0.0 copy-done
  49.6 104.9 %conditional.1 = (bf16[6,48,2,128,128]{4,3,2,1,0:T(8,128)(2,1)}) conditional(s32[]{:T(128)} %bitcast.3, (s32[16,128]{1,0:T(8,128)S(1)}, bf16[8,3,4,4,16,128]{5,4,3,2,1,0:T(8,128)(2,1)S(1)}, bf16[464,512]{1,0:T(8,128)(2,1)S(1)}, s32[12,3]{1,0:T(8,128)S(1)}, s32[6]{0:T(128)S(1)}) %tuple.35, (s32[16,128]{1,0:T(8,128)S(1)}, ...), branch_computations={%region_3.4_spmd, %region_4.5_spmd, %region_5.6_spmd, %region_6.7_... | conditional | bytes 72990728 | solution.py:578
  49.6 90.7 %branch_0_fun.2.left_ref.right_ref = bf16[31,4,464,128]{3,2,1,0:T(8,128)(2,1)S(1)} custom-call(s32[16,128]{1,0:T(8,128)S(1)} %get-tuple-element.50.table_ref, bf16[8,3,4,4,16,128]{5,4,3,2,1,0:T(8,128)(2,1)S(1)} %get-tuple-element.51.white_ref, bf16[464,512]{1,0:T(8,128)(2,1)S(1)} %get-tuple-element.52.pick_ref), custom_call_target="tpu_custom_call" | custom-call | tf_op jit(solution)/shard_map/cond/branch_0_fun/pallas_call | solution.py:522
  140.3 14.2 %branch_0_fun.3 = bf16[6,48,2,128,128]{4,3,2,1,0:T(8,128)(2,1)} custom-call(s32[12,3]{1,0:T(8,128)S(1)} %get-tuple-element.46.needed_ref, s32[6]{0:T(128)S(1)} %get-tuple-element.48.live_ref, bf16[31,4,464,128]{3,2,1,0:T(8,128)(2,1)S(1)} %branch_0_fun.2.left_ref.right_ref, bf16[31,4,464,128]{3,2,1,0:T(8,128)(2,1)S(1)} %branch_0_fun.2.left_ref.right_ref), custom_call_target="tpu_custom_call" | custom-call | tf_op jit(solution)/shard_map/cond/branch_0_fun/pallas_call | solution.py:616
  (4 shorter events, 0.0 us)
Async XLA Ops:
  0.0 49.6 %copy-start = (bf16[464,512]{1,0:T(8,128)(2,1)S(1)}, bf16[464,512]{1,0:T(8,128)(2,1)}, u32[]{:S(2)}) copy-start(bf16[464,512]{1,0:T(8,128)(2,1)} %constant.56.clone) | copy-start | bytes 1425412
  2.8 30.8 %all-to-all-start.2 = ((f16[128,16,256]{2,1,0:T(8,128)(2,1)}), f16[128,16,256]{2,1,0:T(8,128)(2,1)S(1)}, u32[]{:S(2)}, u32[]{:S(2)}) async-start(f16[128,16,256]{2,1,0:T(8,128)(2,1)} %bitcast.6), calls=%async_computation.2 | async-start | bytes 2097152 | tf_op jit(solution)/shard_map/all_to_all | solution.py:641
  18.2 0.8 copy-start.1

commit v6 on v5

--- a/solution.py
+++ b/solution.py
@@ -20,7 +20,7 @@
 QUAD = 4
 VMEM_LIMIT = 56 * 1024 * 1024
 EXCHANGE_LIMIT = 28 * 1024 * 1024
-PRODUCT_LIMIT = 12 * 1024 * 1024
+PRODUCT_LIMIT = 16 * 1024 * 1024
 THIRDS = 3
 STREAMS = 4
 DELAYS = (0, 0, 1, 1)
@@ -578,31 +578,35 @@
     return lax.switch(which, branches)
 
 
-def product_kernel(needed_ref, live_ref, left_ref, right_ref, out_ref):
+def product_kernel(needed_ref, live_ref, *refs):
     slot = pl.program_id(0)
-    streams, rows, block = left_ref.shape[1:]
+    lefts, rights, out_ref = refs[:THIRDS], refs[THIRDS : 2 * THIRDS], refs[-1]
+    streams, rows, block = lefts[0].shape[1:]
     norm = 1.0 / math.sqrt(SEG)
     dims = (((0,), (0,)), ((), ()))
     per = rows // (QUAD * KROWS)
+    quads = streams * per
 
     @pl.when(live_ref[slot] != 0)
     def _():
-        def one(g, carry):
-            at = pl.ds(pl.multiple_of(g % per * (QUAD * KROWS), 16), QUAD * KROWS)
-            left4 = left_ref[0, g // per, at]
-            right4 = right_ref[0, g // per, at]
-            for q in range(QUAD):
-                left = left4[q * KROWS : (q + 1) * KROWS]
-                right = right4[q * KROWS : (q + 1) * KROWS]
-                turned = jnp.concatenate([-right[SEG:], right[:SEG]], axis=0)
-                both = jnp.concatenate([right, turned], axis=1)
-                value = lax.dot_general(left, both, dims, preferred_element_type=jnp.float32)
-                value = (value * norm).astype(jnp.bfloat16)
-                out_ref[0, g * QUAD + q, 0] = value[:, :block]
-                out_ref[0, g * QUAD + q, 1] = value[:, block:]
-            return carry
-
-        lax.fori_loop(0, streams * per, one, 0, unroll=True)
+        for s in range(THIRDS):
+
+            def one(g, carry):
+                at = pl.ds(pl.multiple_of(g % per * (QUAD * KROWS), 16), QUAD * KROWS)
+                left4 = lefts[s][0, g // per, at]
+                right4 = rights[s][0, g // per, at]
+                for q in range(QUAD):
+                    left = left4[q * KROWS : (q + 1) * KROWS]
+                    right = right4[q * KROWS : (q + 1) * KROWS]
+                    turned = jnp.concatenate([-right[SEG:], right[:SEG]], axis=0)
+                    both = jnp.concatenate([right, turned], axis=1)
+                    value = lax.dot_general(left, both, dims, preferred_element_type=jnp.float32)
+                    value = (value * norm).astype(jnp.bfloat16)
+                    out_ref[0, (s * quads + g) * QUAD + q, 0] = value[:, :block]
+                    out_ref[0, (s * quads + g) * QUAD + q, 1] = value[:, block:]
+                return carry
+
+            lax.fori_loop(0, quads, one, 0, unroll=True)
 
     @pl.when(live_ref[slot] == 0)
     def _():
@@ -611,22 +615,23 @@
 
 def products(held, needed, live):
     _, streams, rows, block = held.shape
-    part = streams * (rows // KROWS)
+    freqs = THIRDS * streams * (rows // KROWS)
     spec = (1, streams, rows, block)
+
+    def take(side, third):
+        return pl.BlockSpec(spec, lambda s, need, live: (need[2 * s + side, third], 0, 0, 0))
+
     return pl.pallas_call(
         product_kernel,
-        out_shape=jax.ShapeDtypeStruct((PMAX, THIRDS * part, 2, block, block), jnp.bfloat16),
+        out_shape=jax.ShapeDtypeStruct((PMAX, freqs, 2, block, block), jnp.bfloat16),
         grid_spec=pltpu.PrefetchScalarGridSpec(
             num_scalar_prefetch=2,
-            grid=(PMAX, THIRDS),
-            in_specs=[
-                pl.BlockSpec(spec, lambda s, g, need, live: (need[2 * s, g], 0, 0, 0)),
-                pl.BlockSpec(spec, lambda s, g, need, live: (need[2 * s + 1, g], 0, 0, 0)),
-            ],
-            out_specs=pl.BlockSpec((1, part, 2, block, block), lambda s, g, need, live: (s, g, 0, 0, 0)),
+            grid=(PMAX,),
+            in_specs=[take(side, third) for side in range(2) for third in range(THIRDS)],
+            out_specs=pl.BlockSpec((1, freqs, 2, block, block), lambda s, need, live: (s, 0, 0, 0, 0)),
         ),
         compiler_params=pltpu.CompilerParams(vmem_limit_bytes=PRODUCT_LIMIT),
-    )(needed, live, held, held)
+    )(needed, live, *[held] * (2 * THIRDS))
 
 
 def body(records, pairs, owners, starts):

time: 154 us -> 150 us (0.974); the launches traced: 155 us -> 149 us
  Pallas kernels: 127 us -> 121 us
    pallas_call x1, Pallas kernels: 14.2 us -> 8.59 us  [products(): pl.pallas_call(product_kernel, out_shape=jax.ShapeDtypeStruct((PMAX, freq...]
where the time goes in v6:
time: 150 us; the launch traced here: 149 us
  Pallas kernels  121 us (81%)
  starting transfers between devices  11.5 us (8%)
  other arithmetic  6.54 us (4%)
  local copies, waits for them, and re-layouts  5.6 us (4%)
  between operations  1.98 us (1%)
  waiting for transfers between devices  1.9 us (1%)
    pallas_call x1, Pallas kernels, exchange(): pl.pallas_call(functools.partial(exchange_kernel, count, bands, rounds),...  90.7 us
    pallas_call x1, Pallas kernels, spectra(): pl.pallas_call(functools.partial(spectra_kernel, chan_count, tm_count), o...  14.3 us
    all_to_all x1, starting transfers between devices, body(): lax.all_to_all(moved, ('chan', 'tm'), split_axis=0, concat_axis=0, tiled=...  11.5 us
    pallas_call x1, Pallas kernels, products(): pl.pallas_call(product_kernel, out_shape=jax.ShapeDtypeStruct((PMAX, freq...  8.59 us
    pallas_call x1, Pallas kernels, plan(): pl.pallas_call(plan_kernel, out_shape=(grid, grid, jax.ShapeDtypeStruct((...  7.73 us
  transfers between devices with their start and end apart: 1, of which 1 were waited for; matrix products, arithmetic and copies ran while one was open for 5% of the time, Pallas kernels for 5%

profile of v6, /device:TPU:1, one launch (start us, length us, event | category | flops | bytes accessed | tf_op | source)
XLA Modules:
  0.0 148.9 jit_solution(6429551376149611667)
XLA Ops:
  0.0 0.0 copy-start
  0.0 2.8 %multiply_convert_fusion = f16[2048,256]{1,0:T(8,128)(2,1)} fusion(f32[2048,256]{1,0:T(8,128)} %param.17), kind=kLoop, calls=%fused_computation.2 | loop fusion | flops 1048576 | bytes 3145728 | tf_op jit(solution)/shard_map/convert_element_type | solution.py:645
  2.8 11.5 %all-to-all-start.2 = ((f16[128,16,256]{2,1,0:T(8,128)(2,1)}), f16[128,16,256]{2,1,0:T(8,128)(2,1)S(1)}, u32[]{:S(2)}, u32[]{:S(2)}) async-start(f16[128,16,256]{2,1,0:T(8,128)(2,1)} %bitcast.6), calls=%async_computation.2 | async-start | bytes 2097152 | tf_op jit(solution)/shard_map/all_to_all | solution.py:646
  14.4 1.3 copy.25.owners_ref
  15.7 0.9 convert_reduce_fusion
  16.6 0.7 multiply_add_fusion
  17.3 0.1 select_reduce_fusion
  17.4 0.1 compare_select_fusion.1
  17.5 0.8 copy.24.pairs_ref
  18.2 0.0 copy-start.1
  18.2 0.6 gather_fusion
  18.8 0.1 add.83
  18.9 0.1 compare_select_fusion
  18.9 0.1 reshape.117
  19.0 0.0 copy-done.1
  19.0 7.7 %shard_map.131 = (s32[16,128]{1,0:T(8,128)S(1)}, s32[16,128]{1,0:T(8,128)}, s32[8,128]{1,0:T(8,128)}) custom-call(s32[48,2]{1,0:T(8,128)} %copy-done.1, s32[48,1]{1,0:T(8,128)} %copy.25.owners_ref, bf16[128,32]{1,0:T(8,128)(2,1)} %constant.18.clone.near_ref, bf16[128,32]{1,0:T(8,128)(2,1)} %constant.52.clone.reach_ref, bf16[32,128]{1,0:T(8,128)(2,1)} %constant.53.clone.shell_ref), custom_call_target="tpu_custom_call" | custom-call | tf_op jit(solution)/shard_map/pallas_call | solution.py:314
  26.8 1.2 slice.3
  29.9 0.7 dynamic-slice_bitcast_fusion
  30.6 0.8 gather_fusion.1
  31.4 0.1 reshape.116
  31.5 0.1 fusion
  31.6 0.1 dynamic-slice_convert_fusion
  31.6 0.1 iota_add_fusion
  31.7 1.9 %all-to-all-done.2 = f16[128,16,256]{2,1,0:T(8,128)(2,1)S(1)} async-done(((f16[128,16,256]{2,1,0:T(8,128)(2,1)}), f16[128,16,256]{2,1,0:T(8,128)(2,1)S(1)}, u32[]{:S(2)}, u32[]{:S(2)}) %all-to-all-start.2) | async-done | bytes 1048608 | tf_op jit(solution)/shard_map/all_to_all | solution.py:646
  33.6 1.6 %convert_element_type.30.rec_ref = f32[128,16,256]{2,1,0:T(8,128)} convert(f16[128,16,256]{2,1,0:T(8,128)(2,1)S(1)} %all-to-all-done.2) | non-fusion elementwise | flops 524288 | bytes 3145728 | tf_op jit(solution)/shard_map/convert_element_type | solution.py:647
  35.2 14.3 %shard_map.132 = bf16[384,16,128]{2,1,0:T(8,128)(2,1)S(1)} custom-call(s32[58]{0:T(128)} %starts_ref.1, f32[128,16,256]{2,1,0:T(8,128)} %convert_element_type.30.rec_ref, bf16[768,1024]{1,0:T(8,128)(2,1)} %constant.54.clone.high_hbm, bf16[768,1024]{1,0:T(8,128)(2,1)} %constant.55.clone.low_hbm), custom_call_target="tpu_custom_call" | custom-call | tf_op jit(solution)/shard_map/pallas_call | solution.py:166
  49.6 0.0 copy-done
  49.6 99.3 %conditional.1 = (bf16[6,48,2,128,128]{4,3,2,1,0:T(8,128)(2,1)}) conditional(s32[]{:T(128)} %bitcast.3, (s32[16,128]{1,0:T(8,128)S(1)}, bf16[8,3,4,4,16,128]{5,4,3,2,1,0:T(8,128)(2,1)S(1)}, bf16[464,512]{1,0:T(8,128)(2,1)S(1)}, s32[12,3]{1,0:T(8,128)S(1)}, s32[6]{0:T(128)S(1)}) %tuple.35, (s32[16,128]{1,0:T(8,128)S(1)}, ...), branch_computations={%region_3.4_spmd, %region_4.5_spmd, %region_5.6_spmd, %region_6.7_... | conditional | bytes 72990728 | solution.py:578
  49.6 90.7 %branch_0_fun.2.refs_0_.refs_1_.refs_2_.refs_3_.refs_4_.refs_5_ = bf16[31,4,464,128]{3,2,1,0:T(8,128)(2,1)S(1)} custom-call(s32[16,128]{1,0:T(8,128)S(1)} %get-tuple-element.50.table_ref, bf16[8,3,4,4,16,128]{5,4,3,2,1,0:T(8,128)(2,1)S(1)} %get-tuple-element.51.white_ref, bf16[464,512]{1,0:T(8,128)(2,1)S(1)} %get-tuple-element.52.pick_ref), custom_call_target="tpu_custom_call" | custom-call | tf_op jit(solution)/shard_map/cond/branch_0_fun/pallas_call | solution.py:522
  140.3 8.6 %branch_0_fun.3 = bf16[6,48,2,128,128]{4,3,2,1,0:T(8,128)(2,1)} custom-call(s32[12,3]{1,0:T(8,128)S(1)} %get-tuple-element.46.needed_ref, s32[6]{0:T(128)S(1)} %get-tuple-element.48.live_ref, bf16[31,4,464,128]{3,2,1,0:T(8,128)(2,1)S(1)} %branch_0_fun.2.refs_0_.refs_1_.refs_2_.refs_3_.refs_4_.refs_5_, ...), custom_call_target="tpu_custom_call" | custom-call | tf_op jit(solution)/shard_map/cond/branch_0_fun/pallas_call | solution.py:624
  (4 shorter events, 0.0 us)
Async XLA Ops:
  0.0 49.6 %copy-start = (bf16[464,512]{1,0:T(8,128)(2,1)S(1)}, bf16[464,512]{1,0:T(8,128)(2,1)}, u32[]{:S(2)}) copy-start(bf16[464,512]{1,0:T(8,128)(2,1)} %constant.56.clone) | copy-start | bytes 1425412
  2.8 30.8 %all-to-all-start.2 = ((f16[128,16,256]{2,1,0:T(8,128)(2,1)}), f16[128,16,256]{2,1,0:T(8,128)(2,1)S(1)}, u32[]{:S(2)}, u32[]{:S(2)}) async-start(f16[128,16,256]{2,1,0:T(8,128)(2,1)} %bitcast.6), calls=%async_computation.2 | async-start | bytes 2097152 | tf_op jit(solution)/shard_map/all_to_all | solution.py:646
  18.2 0.8 copy-start.1
